TPU v7x, 32 devices: a whole 2x2x4 slice. The times are simulated.
32 devices in a mesh: tile: 16 (over z, x, core), head: 2 (over y).
Axes of the slice: x: 2, y: 2, z: 4, core: 2. Of those that a mesh axis runs over, the one named last changes fastest.
Arguments:
- queries: bfloat16 [16384, 768], P(('tile', 'head')), may hold values from -16 to 16
- keys_in: bfloat16 [16384, 768], P(('tile', 'head')), may hold values from -16 to 16
- values_in: bfloat16 [16384, 768], P(('tile', 'head')), may hold values from -6 to 6
- grad_out: bfloat16 [16384, 768], P(('tile', 'head')), may hold values from -6 to 6
- positions: int32 [2, 16384], P(None, ('tile', 'head')), may hold values from 0 to 255
Outputs:
- attended: bfloat16 [16384, 768], P(('tile', 'head'))
- query_grad: bfloat16 [16384, 768], P(('tile', 'head'))
- key_grad: bfloat16 [16384, 768], P(('tile', 'head'))
- value_grad: bfloat16 [16384, 768], P(('tile', 'head'))
All inputs are finite; a program needn't handle non-finite values.
Results may differ from a plain program's by a relative error of at most 0.011.
Values may be sent and summed in bfloat16 or wider, within the bound.
A program may use at most 128 MiB of HBM per device.

v0:
```python
import math

import jax
import jax.numpy as jnp
from jax import lax
from jax.sharding import PartitionSpec as P

HEAD_DIM = 128
TILE_TOK = 256
GRID_COLS = 8


THETA = 10000.0


def as_sent(value):
    return jax.tree.map(lambda a: a.astype(jnp.bfloat16) if a.dtype == jnp.float32 else a, value)


def passed_along(value, axis, by):
    count = lax.axis_size(axis)
    pairs = [(i, i + by) for i in range(count) if 0 <= i + by < count]
    return lax.ppermute(value, axis, pairs)


def angle_tables(row_ids, col_ids):
    turned = 7 * HEAD_DIM // 16
    unturned = HEAD_DIM - 2 * turned
    slot_ids = lax.iota(jnp.int32, HEAD_DIM)
    offset = slot_ids - unturned
    by_column = offset >= turned
    within = jnp.where(by_column, offset - turned, offset)
    paired = jnp.maximum(within, 0) // 2
    frequency = jnp.exp(paired.astype(jnp.float32) * (-2.0 * math.log(THETA) / turned))
    chosen = jnp.where(by_column[None, :], col_ids[:, None], row_ids[:, None]).astype(jnp.float32)
    angles = chosen * frequency[None, :]
    active = (offset >= 0)[None, :]
    cosine = jnp.where(active, jnp.cos(angles), 1.0)
    parity = jnp.where(within % 2 == 0, -1.0, 1.0)
    signed_sine = jnp.where(active, jnp.sin(angles) * parity[None, :], 0.0)
    return (cosine, signed_sine)


def swap_matrix():
    slot_ids = lax.iota(jnp.int32, HEAD_DIM)
    partner = jnp.bitwise_xor(slot_ids, 1)
    return (slot_ids[:, None] == partner[None, :]).astype(jnp.float32)


def turn_forward(tensor, cosine, signed_sine, matrix):
    flattened = tensor.reshape(-1, HEAD_DIM)
    swapped = jnp.dot(flattened, matrix, precision=lax.Precision.HIGHEST).reshape(tensor.shape)
    return tensor * cosine[:, None, :] + swapped * signed_sine[:, None, :]


def turn_back(gradient, cosine, signed_sine, matrix):
    flattened = (gradient * signed_sine[:, None, :]).reshape(-1, HEAD_DIM)
    swapped = jnp.dot(flattened, matrix, precision=lax.Precision.HIGHEST).reshape(gradient.shape)
    return gradient * cosine[:, None, :] + swapped


def send_tiles(first_part, second_part, stride):
    return (
        passed_along(as_sent(first_part), "tile", stride).astype(first_part.dtype),
        passed_along(as_sent(second_part), "tile", stride).astype(second_part.dtype),
    )


def send_sums(first_part, second_part, stride):
    return (
        passed_along(as_sent(first_part), "tile", stride).astype(first_part.dtype),
        passed_along(as_sent(second_part), "tile", stride).astype(second_part.dtype),
    )


def band_plan(number, reach_tiles):
    used_slots = sorted(
        {
            local_tile + reach_tiles + row_step * GRID_COLS + col_step
            for local_tile in range(number)
            for row_step in (-1, 0, 1)
            for col_step in (-1, 0, 1)
        }
    )
    send_plan = {}
    for slot_at in used_slots:
        if slot_at < reach_tiles:
            stride = -(-(reach_tiles - slot_at) // number)
            if stride not in send_plan:
                send_plan[stride] = []
            send_plan[stride].append((slot_at, slot_at - reach_tiles + stride * number))
        elif slot_at >= reach_tiles + number:
            beyond = slot_at - reach_tiles - number
            stride = beyond // number + 1
            if -stride not in send_plan:
                send_plan[-stride] = []
            send_plan[-stride].append((slot_at, beyond - (stride - 1) * number))
    return send_plan


def chosen_tiles(tensor, tile_list, axis_dim):
    return jnp.concatenate(
        [
            lax.slice_in_dim(tensor, tile_at * TILE_TOK, (tile_at + 1) * TILE_TOK, axis=axis_dim)
            for tile_at in tile_list
        ],
        axis=axis_dim,
    )


def tile_band(first_part, second_part, axis_dim, reach_tiles, sender):
    length = first_part.shape[axis_dim]
    number = length // TILE_TOK
    send_plan = band_plan(number, reach_tiles)
    received = {}
    for stride in sorted(send_plan):
        entries = send_plan[stride]
        tile_list = [entry[1] for entry in entries]
        arrived = sender(
            chosen_tiles(first_part, tile_list, axis_dim),
            chosen_tiles(second_part, tile_list, axis_dim),
            stride,
        )
        for member, entry in enumerate(entries):
            received[entry[0]] = (
                lax.slice_in_dim(
                    arrived[0], member * TILE_TOK, (member + 1) * TILE_TOK, axis=axis_dim
                ),
                lax.slice_in_dim(
                    arrived[1], member * TILE_TOK, (member + 1) * TILE_TOK, axis=axis_dim
                ),
            )
    first_shape = list(first_part.shape)
    first_shape[axis_dim] = TILE_TOK
    second_shape = list(second_part.shape)
    second_shape[axis_dim] = TILE_TOK
    empty_pair = (
        jnp.zeros(tuple(first_shape), first_part.dtype),
        jnp.zeros(tuple(second_shape), second_part.dtype),
    )
    first_pieces = []
    second_pieces = []
    for slot_at in (
        list(range(reach_tiles))
        + [-1]
        + list(range(reach_tiles + number, 2 * reach_tiles + number))
    ):
        if slot_at < 0:
            first_pieces.append(first_part)
            second_pieces.append(second_part)
        else:
            chosen_pair = received[slot_at] if slot_at in received else empty_pair
            first_pieces.append(chosen_pair[0])
            second_pieces.append(chosen_pair[1])
    return (
        jnp.concatenate(first_pieces, axis=axis_dim),
        jnp.concatenate(second_pieces, axis=axis_dim),
    )


def fold_band(first_band, second_band, reach_tiles, sender):
    margin = reach_tiles * TILE_TOK
    length = first_band.shape[0] - 2 * margin
    number = length // TILE_TOK
    send_plan = band_plan(number, reach_tiles)
    first_tiles = [
        first_band[margin + tile_at * TILE_TOK : margin + (tile_at + 1) * TILE_TOK]
        for tile_at in range(number)
    ]
    second_tiles = [
        second_band[margin + tile_at * TILE_TOK : margin + (tile_at + 1) * TILE_TOK]
        for tile_at in range(number)
    ]
    for stride in sorted(send_plan):
        entries = send_plan[stride]
        slot_list = [entry[0] for entry in entries]
        arrived = sender(
            chosen_tiles(first_band, slot_list, 0), chosen_tiles(second_band, slot_list, 0), -stride
        )
        for member, entry in enumerate(entries):
            first_tiles[entry[1]] = (
                first_tiles[entry[1]] + arrived[0][member * TILE_TOK : (member + 1) * TILE_TOK]
            )
            second_tiles[entry[1]] = (
                second_tiles[entry[1]] + arrived[1][member * TILE_TOK : (member + 1) * TILE_TOK]
            )
    return (jnp.concatenate(first_tiles, axis=0), jnp.concatenate(second_tiles, axis=0))


def query_kernel(q_tile, g_tile, near_keys, near_values, usable):
    inv_root = HEAD_DIM ** (-0.5)
    scores = (
        jnp.einsum("qhd,khd->hqk", q_tile, near_keys, preferred_element_type=jnp.float32) * inv_root
    )
    scores = jnp.where(usable[None, None, :], scores, -jnp.inf)
    row_max = jnp.max(scores, axis=-1, keepdims=True)
    log_norm = row_max + jnp.log(jnp.sum(jnp.exp(scores - row_max), axis=-1, keepdims=True))
    weights = jnp.exp(scores - log_norm)
    weights_half = weights.astype(jnp.bfloat16)
    attended = jnp.einsum(
        "hqk,khd->qhd", weights_half, near_values, preferred_element_type=jnp.float32
    ).astype(jnp.bfloat16)
    row_dots = jnp.sum(g_tile.astype(jnp.float32) * attended.astype(jnp.float32), axis=-1).T
    weight_grad = jnp.einsum(
        "qhd,khd->hqk", g_tile, near_values, preferred_element_type=jnp.float32
    )
    dscore = (weights * (weight_grad - row_dots[:, :, None]) * inv_root).astype(jnp.bfloat16)
    dq_rot = jnp.einsum("hqk,khd->qhd", dscore, near_keys, preferred_element_type=jnp.float32)
    dk_part = jnp.einsum("hqk,qhd->khd", dscore, q_tile, preferred_element_type=jnp.float32)
    dv_part = jnp.einsum("hqk,qhd->khd", weights_half, g_tile, preferred_element_type=jnp.float32)
    return (attended, log_norm[:, :, 0], row_dots, dq_rot, dk_part, dv_part)


def local(queries, keys_in, values_in, grad_out, positions):
    grid_ids = lax.all_gather(positions, "head", axis=1, tiled=True)
    q_raw, k_raw, v_raw, g_raw = (
        lax.all_to_all(queries, "head", split_axis=1, concat_axis=0, tiled=True),
        lax.all_to_all(keys_in, "head", split_axis=1, concat_axis=0, tiled=True),
        lax.all_to_all(values_in, "head", split_axis=1, concat_axis=0, tiled=True),
        lax.all_to_all(grad_out, "head", split_axis=1, concat_axis=0, tiled=True),
    )
    row_count = q_raw.shape[0]
    head_count = q_raw.shape[1] // HEAD_DIM
    number = row_count // TILE_TOK
    shape_here = (row_count, head_count, HEAD_DIM)
    cosine, signed_sine = angle_tables(grid_ids[0], grid_ids[1])
    matrix = swap_matrix()
    q_rot = turn_forward(
        q_raw.astype(jnp.float32).reshape(shape_here), cosine, signed_sine, matrix
    ).astype(jnp.bfloat16)
    k_rot = turn_forward(
        k_raw.astype(jnp.float32).reshape(shape_here), cosine, signed_sine, matrix
    ).astype(jnp.bfloat16)
    values = v_raw.reshape(shape_here)
    grads = g_raw.reshape(shape_here)
    reach_tiles = GRID_COLS + 1
    first_tile = lax.axis_index("tile") * number
    grid_rows = lax.axis_size("tile") * number // GRID_COLS
    keys_band, values_band = tile_band(k_rot, values, 0, reach_tiles, send_tiles)

    def near_flags(local_tile):
        global_tile = first_tile + local_tile
        row_of = global_tile // GRID_COLS
        col_of = global_tile % GRID_COLS
        offsets = []
        flag_list = []
        for row_step in (-1, 0, 1):
            for col_step in (-1, 0, 1):
                offsets.append(local_tile + reach_tiles + row_step * GRID_COLS + col_step)
                near_flag = (
                    (row_of + row_step >= 0)
                    & (row_of + row_step < grid_rows)
                    & (col_of + col_step >= 0)
                    & (col_of + col_step < GRID_COLS)
                )
                flag_list.append(jnp.broadcast_to(near_flag, (TILE_TOK,)))
        return (offsets, jnp.concatenate(flag_list))

    def pick_near(band, offsets, axis_dim):
        return jnp.concatenate(
            [
                lax.dynamic_slice_in_dim(band, offset * TILE_TOK, TILE_TOK, axis_dim)
                for offset in offsets
            ],
            axis=axis_dim,
        )

    def own_tile(tensor, local_tile):
        return lax.dynamic_slice_in_dim(tensor, local_tile * TILE_TOK, TILE_TOK, 0)

    def put_tile(tensor, piece, local_tile, axis_dim):
        return lax.dynamic_update_slice_in_dim(tensor, piece, local_tile * TILE_TOK, axis_dim)

    def add_near(band, terms, offsets):
        for member, offset in enumerate(offsets):
            start_at = offset * TILE_TOK
            current = lax.dynamic_slice_in_dim(band, start_at, TILE_TOK, 0)
            band = lax.dynamic_update_slice_in_dim(
                band, current + terms[member * TILE_TOK : (member + 1) * TILE_TOK], start_at, 0
            )
        return band

    start_state = (
        jnp.zeros(shape_here, jnp.bfloat16),
        jnp.zeros((head_count, row_count), jnp.float32),
        jnp.zeros((head_count, row_count), jnp.float32),
        jnp.zeros(shape_here, jnp.float32),
    )
    band_shape = (keys_band.shape[0], head_count, HEAD_DIM)
    start_state = start_state + (
        jnp.zeros(band_shape, jnp.float32),
        jnp.zeros(band_shape, jnp.float32),
    )

    def query_step(local_tile, buffers):
        offsets, usable = near_flags(local_tile)
        results = query_kernel(
            own_tile(q_rot, local_tile),
            own_tile(grads, local_tile),
            pick_near(keys_band, offsets, 0),
            pick_near(values_band, offsets, 0),
            usable,
        )
        updated = (
            put_tile(buffers[0], results[0], local_tile, 0),
            put_tile(buffers[1], results[1], local_tile, 1),
            put_tile(buffers[2], results[2], local_tile, 1),
            put_tile(buffers[3], results[3], local_tile, 0),
        )
        updated = updated + (
            add_near(buffers[4], results[4], offsets),
            add_near(buffers[5], results[5], offsets),
        )
        return updated

    buffers = lax.fori_loop(0, number, query_step, start_state)
    attended, log_norm, row_dots, dq_rot = (buffers[0], buffers[1], buffers[2], buffers[3])
    dk_rot, dv_sum = fold_band(buffers[4], buffers[5], reach_tiles, send_sums)
    query_grad = (
        turn_back(dq_rot, cosine, signed_sine, matrix).astype(jnp.bfloat16).reshape(row_count, -1)
    )
    key_grad = (
        turn_back(dk_rot, cosine, signed_sine, matrix).astype(jnp.bfloat16).reshape(row_count, -1)
    )
    value_grad = dv_sum.astype(jnp.bfloat16).reshape(row_count, -1)
    return (
        lax.all_to_all(
            as_sent(attended.reshape(row_count, -1)),
            "head",
            split_axis=0,
            concat_axis=1,
            tiled=True,
        ),
        lax.all_to_all(query_grad, "head", split_axis=0, concat_axis=1, tiled=True),
        lax.all_to_all(key_grad, "head", split_axis=0, concat_axis=1, tiled=True),
        lax.all_to_all(value_grad, "head", split_axis=0, concat_axis=1, tiled=True),
    )


def solution(mesh):
    placed = (
        P(("tile", "head"), None),
        P(("tile", "head"), None),
        P(("tile", "head"), None),
        P(("tile", "head"), None),
        P(None, ("tile", "head")),
    )
    return jax.shard_map(
        local,
        mesh=mesh,
        in_specs=placed,
        out_specs=(
            P(("tile", "head"), None),
            P(("tile", "head"), None),
            P(("tile", "head"), None),
            P(("tile", "head"), None),
        ),
        check_vma=False,
    )
```

profile of v0, /device:TPU:16, one launch (start us, length us, event | category | flops | bytes accessed | tf_op | source)
XLA Modules:
  0.0 655.1 jit_solution(18005531831902921391)
XLA Ops:
  2.8 3.5 all-to-all-start.1
  8.5 9.1 %all_gather.3 = s32[2,1024]{1,0:T(2,128)S(1)} all-gather(s32[2,512]{1,0:T(2,128)S(1)} %copy-done.16), channel_id=1, replica_groups=mesh['tile'=16,'head'=2] {'head'}, dimensions={1}, use_global_device_ids=true | all-gather | bytes 12288 | tf_op jit(solution)/shard_map/all_gather | solution.py:215
  17.6 3.5 all-to-all-start.2
  24.6 3.0 cosine_select_fusion
  28.0 3.2 all-to-all-done.2
  31.2 4.3 all-to-all-start
  37.1 3.0 copy.140
  47.6 3.0 copy.145
  50.6 3.7 reshape.284
  54.3 4.4 all-to-all-start.3
  61.5 3.2 reshape.282
  67.2 3.6 reshape.290
  72.1 3.6 reshape.289
  75.7 4.7 fusion.31
  80.4 3.4 collective-permute-start.7
  83.8 3.4 collective-permute-start.1
  99.2 24.9 %collective-permute-done.6 = bf16[256,3,128]{2,0,1:T(8,128)(2,1)} collective-permute-done((bf16[256,3,128]{2,0,1:T(8,128)(2,1)S(1)}, bf16[256,3,128]{2,0,1:T(8,128)(2,1)}, u32[]{:S(2)}, u32[]{:S(2)}) %collective-permute-start.6) | collective-permute-done | bytes 196640 | tf_op jit(solution)/shard_map/ppermute | solution.py:23
  124.2 7.1 %collective-permute-start.5 = (bf16[256,3,128]{0,2,1:T(8,128)(2,1)S(1)}, bf16[256,3,128]{0,2,1:T(8,128)(2,1)S(1)}, u32[]{:S(2)}, u32[]{:S(2)}) collective-permute-start(bf16[256,3,128]{0,2,1:T(8,128)(2,1)S(1)} %get-tuple-element.439), channel_id=1, source_target_pairs={{6,0},{8,2},{10,4},{12,6},{14,8},{16,10},{18,12},{20,14},{22,16},{... | collective-permute-start | bytes 589832 | tf_op jit(solution)/shard_map/ppermute | solution.py:23
  150.6 3.1 collective-permute-start.9
  158.1 11.5 %collective-permute-done.9 = bf16[512,3,128]{2,0,1:T(8,128)(2,1)S(1)} collective-permute-done((bf16[512,3,128]{2,0,1:T(8,128)(2,1)}, bf16[512,3,128]{2,0,1:T(8,128)(2,1)S(1)}, u32[]{:S(2)}, u32[]{:S(2)}) %collective-permute-start.9) | collective-permute-done | bytes 393248 | tf_op jit(solution)/shard_map/ppermute | solution.py:23
  169.6 4.4 collective-permute-start.10
  178.7 13.2 %collective-permute-done.10 = bf16[1024,3,128]{2,0,1:T(8,128)(2,1)S(1)} collective-permute-done((bf16[1024,3,128]{2,0,1:T(8,128)(2,1)}, bf16[1024,3,128]{2,0,1:T(8,128)(2,1)S(1)}, u32[]{:S(2)}, u32[]{:S(2)}) %collective-permute-start.10) | collective-permute-done | bytes 786464 | tf_op jit(solution)/shard_map/ppermute | solution.py:23
  198.3 4.5 broadcast.233.clone
  202.7 4.4 broadcast.233
  207.2 296.2 %while.24 = (s32[]{:T(128)}, bf16[1024,3,128]{0,2,1:T(8,128)(2,1)}, f32[1024,3,128]{2,0,1:T(8,128)}, f32[5632,3,128]{0,2,1:T(8,128)}, f32[5632,3,128]{0,2,1:T(8,...) while((s32[]{:T(128)}, bf16[1024,3,128]{0,2,1:T(8,128)(2,1)}, ...), condition=%wide.region_4.5_spmd, body=%wide.region_0.4_spmd.sunk | while | flops 2744941056 | bytes 106212480 | solution.py:316
  235.6 4.2 convolution_bitcast_fusion.9
  304.6 3.0 multiply_convert_fusion.2
  307.5 4.2 convolution_bitcast_fusion.9
  376.4 3.0 multiply_convert_fusion.2
  379.4 4.2 convolution_bitcast_fusion.9
  448.1 3.0 multiply_convert_fusion.2
  451.1 4.2 convolution_bitcast_fusion.9
  503.4 3.9 convert.47
  512.9 3.9 collective-permute-start.21
  516.8 4.4 collective-permute-start.19
  523.6 9.1 %copy.155 = f32[5632,3,128]{2,0,1:T(8,128)} copy(f32[5632,3,128]{0,2,1:T(8,128)} %get-tuple-element.371) | data formatting | bytes 17301504 | tf_op jit(solution)/shard_map/while | solution.py:316
  532.7 4.0 convert.46
  543.6 4.4 collective-permute-start.15
  552.3 4.3 all-to-all-start.4
  561.9 11.1 %collective-permute-start.16 = (bf16[1024,3,128]{2,0,1:T(8,128)(2,1)}, bf16[1024,3,128]{2,0,1:T(8,128)(2,1)}, u32[]{:S(2)}, u32[]{:S(2)}) collective-permute-start(bf16[1024,3,128]{2,0,1:T(8,128)(2,1)} %get-tuple-element.434), channel_id=1, source_target_pairs={{4,0},{6,2},{8,4},{10,6},{12,8},{14,10},{16,12},{18,14},{20,16},{2... | collective-permute-start | bytes 2359304 | tf_op jit(solution)/shard_map/ppermute | solution.py:23
  573.0 9.4 %collective-permute-start.18 = (bf16[256,3,128]{0,2,1:T(8,128)(2,1)}, bf16[256,3,128]{0,2,1:T(8,128)(2,1)}, u32[]{:S(2)}, u32[]{:S(2)}) collective-permute-start(bf16[256,3,128]{0,2,1:T(8,128)(2,1)} %get-tuple-element.419), channel_id=1, source_target_pairs={{0,6},{2,8},{4,10},{6,12},{8,14},{10,16},{12,18},{14,20},{16,22},{... | collective-permute-start | bytes 589832 | tf_op jit(solution)/shard_map/ppermute | solution.py:23
  582.4 8.9 %collective-permute-start.23 = (bf16[256,3,128]{0,2,1:T(8,128)(2,1)}, bf16[256,3,128]{0,2,1:T(8,128)(2,1)}, u32[]{:S(2)}, u32[]{:S(2)}) collective-permute-start(bf16[256,3,128]{0,2,1:T(8,128)(2,1)} %get-tuple-element.420), channel_id=1, source_target_pairs={{6,0},{8,2},{10,4},{12,6},{14,8},{16,10},{18,12},{20,14},{22,16},{... | collective-permute-start | bytes 589832 | tf_op jit(solution)/shard_map/ppermute | solution.py:23
  606.5 4.3 all-to-all-start.5
  610.9 5.2 collective-permute-start.17
  622.4 4.3 all-to-all-start.7
  631.9 7.0 %all-to-all-done.7 = bf16[2,512,384]{2,1,0:T(8,128)(2,1)} async-done(((bf16[2,512,384]{2,1,0:T(8,128)(2,1)}), bf16[2,512,384]{2,1,0:T(8,128)(2,1)}, u32[]{:S(2)}, u32[]{:S(2)}) %all-to-all-start.7) | async-done | bytes 786464 | tf_op jit(solution)/shard_map/all_to_all | solution.py:336
  638.9 3.5 all-to-all-start.6
  649.9 3.9 all-to-all-done.6
  (409 shorter events, 390.7 us)
Async XLA Ops:
  0.6 7.8 %copy-start.16 = (s32[2,512]{1,0:T(2,128)S(1)}, s32[2,512]{1,0:T(2,128)}, u32[]{:S(2)}) copy-start(s32[2,512]{1,0:T(2,128)} %param.11) | copy-start | bytes 12292
  0.6 20.5 %copy-start.10 = (bf16[512,768]{1,0:T(8,128)(2,1)S(1)}, bf16[512,768]{1,0:T(8,128)(2,1)}, u32[]{:S(2)}) copy-start(bf16[512,768]{1,0:T(8,128)(2,1)} %param.9) | copy-start | bytes 2359300
  2.8 14.8 %all-to-all-start.1 = ((bf16[512,2,384]{2,0,1:T(8,128)(2,1)}), bf16[512,2,384]{2,0,1:T(8,128)(2,1)S(1)}, u32[]{:S(2)}, u32[]{:S(2)}) async-start(bf16[512,2,384]{2,0,1:T(8,128)(2,1)} %bitcast.68), calls=%async_computation.1 | async-start | bytes 1572864 | tf_op jit(solution)/shard_map/all_to_all | solution.py:217
  17.6 13.6 %all-to-all-start.2 = ((bf16[512,2,384]{2,0,1:T(8,128)(2,1)}), bf16[512,2,384]{2,0,1:T(8,128)(2,1)S(1)}, u32[]{:S(2)}, u32[]{:S(2)}) async-start(bf16[512,2,384]{2,0,1:T(8,128)(2,1)} %bitcast.67), calls=%async_computation.2 | async-start | bytes 1572864 | tf_op jit(solution)/shard_map/all_to_all | solution.py:218
  21.1 23.8 %copy-start.14 = (s32[128]{0:T(128)}, s32[128]{0:T(128)S(1)}, u32[]{:S(2)}) copy-start(s32[128]{0:T(128)S(1)} %iota_xor_fusion) | copy-start | bytes 1540
  27.7 48.1 %copy-start.5 = (f32[1024,128]{1,0:T(8,128)}, f32[1024,128]{1,0:T(8,128)S(1)}, u32[]{:S(2)}) copy-start(f32[1024,128]{1,0:T(8,128)S(1)} %get-tuple-element.441) | copy-start | bytes 1572868
  31.2 5.9 copy-start.2
  31.2 23.1 %all-to-all-start = ((bf16[512,2,384]{0,2,1:T(8,128)(2,1)}), bf16[512,2,384]{0,2,1:T(8,128)(2,1)}, u32[]{:S(2)}, u32[]{:S(2)}) async-start(bf16[512,2,384]{0,2,1:T(8,128)(2,1)} %bitcast.93), calls=%async_computation | async-start | bytes 1572864 | tf_op jit(solution)/shard_map/all_to_all | solution.py:219
  54.3 41.5 %all-to-all-start.3 = ((bf16[512,2,384]{0,2,1:T(8,128)(2,1)}), bf16[512,2,384]{0,2,1:T(8,128)(2,1)}, u32[]{:S(2)}, u32[]{:S(2)}) async-start(bf16[512,2,384]{0,2,1:T(8,128)(2,1)} %bitcast.91), calls=%async_computation.3 | async-start | bytes 1572864 | tf_op jit(solution)/shard_map/all_to_all | solution.py:220
  75.7 8.1 %copy-start.4 = (bf16[1024,3,128]{0,2,1:T(8,128)(2,1)S(1)}, bf16[1024,3,128]{0,2,1:T(8,128)(2,1)}, u32[]{:S(2)}) copy-start(bf16[1024,3,128]{0,2,1:T(8,128)(2,1)} %reshape.282) | copy-start | bytes 2359300
  80.4 55.3 %collective-permute-start.7 = (bf16[1024,3,128]{2,0,1:T(8,128)(2,1)}, bf16[1024,3,128]{2,0,1:T(8,128)(2,1)}, u32[]{:S(2)}, u32[]{:S(2)}) collective-permute-start(bf16[1024,3,128]{2,0,1:T(8,128)(2,1)} %get-tuple-element.435), channel_id=1, source_target_pairs={{0,4},{2,6},{4,8},{6,10},{8,12},{10,14},{12,16},{14,18},{16,20},{1... | collective-permute-start | bytes 2359304 | tf_op jit(solution)/shard_map/ppermute | solution.py:23
  83.8 61.8 %collective-permute-start.1 = (bf16[1024,3,128]{0,2,1:T(8,128)(2,1)S(1)}, bf16[1024,3,128]{0,2,1:T(8,128)(2,1)S(1)}, u32[]{:S(2)}, u32[]{:S(2)}) collective-permute-start(bf16[1024,3,128]{0,2,1:T(8,128)(2,1)S(1)} %copy-done.4), channel_id=1, source_target_pairs={{0,4},{2,6},{4,8},{6,10},{8,12},{10,14},{12,16},{14,18},{16,20},{1... | collective-permute-start | bytes 2359304 | tf_op jit(solution)/shard_map/ppermute | solution.py:23
  87.3 45.7 %collective-permute-start = (bf16[256,3,128]{0,2,1:T(8,128)(2,1)S(1)}, bf16[256,3,128]{0,2,1:T(8,128)(2,1)S(1)}, u32[]{:S(2)}, u32[]{:S(2)}) collective-permute-start(bf16[256,3,128]{0,2,1:T(8,128)(2,1)S(1)} %get-tuple-element.440), channel_id=1, source_target_pairs={{0,6},{2,8},{4,10},{6,12},{8,14},{10,16},{12,18},{14,20},{16,22},{... | collective-permute-start | bytes 589832 | tf_op jit(solution)/shard_map/ppermute | solution.py:23
  90.3 33.9 %collective-permute-start.6 = (bf16[256,3,128]{2,0,1:T(8,128)(2,1)S(1)}, bf16[256,3,128]{2,0,1:T(8,128)(2,1)}, u32[]{:S(2)}, u32[]{:S(2)}) collective-permute-start(bf16[256,3,128]{2,0,1:T(8,128)(2,1)S(1)} %get-tuple-element.438), channel_id=1, source_target_pairs={{0,6},{2,8},{4,10},{6,12},{8,14},{10,16},{12,18},{14,20},{16,22},{... | collective-permute-start | bytes 589832 | tf_op jit(solution)/shard_map/ppermute | solution.py:23
  93.0 47.3 %collective-permute-start.8 = (bf16[512,3,128]{2,0,1:T(8,128)(2,1)}, bf16[512,3,128]{2,0,1:T(8,128)(2,1)}, u32[]{:S(2)}, u32[]{:S(2)}) collective-permute-start(bf16[512,3,128]{2,0,1:T(8,128)(2,1)} %pad_maximum_fusion.4), channel_id=1, source_target_pairs={{0,2},{2,4},{4,6},{6,8},{8,10},{10,12},{12,14},{14,16},{16,18},{18... | collective-permute-start | bytes 1179656 | tf_op jit(solution)/shard_map/ppermute | solution.py:23
  124.2 71.2 %collective-permute-start.5 = (bf16[256,3,128]{0,2,1:T(8,128)(2,1)S(1)}, bf16[256,3,128]{0,2,1:T(8,128)(2,1)S(1)}, u32[]{:S(2)}, u32[]{:S(2)}) collective-permute-start(bf16[256,3,128]{0,2,1:T(8,128)(2,1)S(1)} %get-tuple-element.439), channel_id=1, source_target_pairs={{6,0},{8,2},{10,4},{12,6},{14,8},{16,10},{18,12},{20,14},{22,16},{... | collective-permute-start | bytes 589832 | tf_op jit(solution)/shard_map/ppermute | solution.py:23
  133.0 43.5 %collective-permute-start.3 = (bf16[512,3,128]{0,2,1:T(8,128)(2,1)}, bf16[512,3,128]{0,2,1:T(8,128)(2,1)S(1)}, u32[]{:S(2)}, u32[]{:S(2)}) collective-permute-start(bf16[512,3,128]{0,2,1:T(8,128)(2,1)} %pad_maximum_fusion.3), channel_id=1, source_target_pairs={{2,0},{4,2},{6,4},{8,6},{10,8},{12,10},{14,12},{16,14},{18,16},{20... | collective-permute-start | bytes 1179656 | tf_op jit(solution)/shard_map/ppermute | solution.py:23
  135.6 15.0 %collective-permute-start.2 = (bf16[512,3,128]{0,2,1:T(8,128)(2,1)}, bf16[512,3,128]{0,2,1:T(8,128)(2,1)S(1)}, u32[]{:S(2)}, u32[]{:S(2)}) collective-permute-start(bf16[512,3,128]{0,2,1:T(8,128)(2,1)} %pad_maximum_fusion.3), channel_id=1, source_target_pairs={{0,2},{2,4},{4,6},{6,8},{8,10},{10,12},{12,14},{14,16},{16,18},{18... | collective-permute-start | bytes 1179656 | tf_op jit(solution)/shard_map/ppermute | solution.py:23
  140.3 54.1 %collective-permute-start.4 = (bf16[1024,3,128]{0,2,1:T(8,128)(2,1)S(1)}, bf16[1024,3,128]{0,2,1:T(8,128)(2,1)S(1)}, u32[]{:S(2)}, u32[]{:S(2)}) collective-permute-start(bf16[1024,3,128]{0,2,1:T(8,128)(2,1)S(1)} %copy-done.4), channel_id=1, source_target_pairs={{4,0},{6,2},{8,4},{10,6},{12,8},{14,10},{16,12},{18,14},{20,16},{2... | collective-permute-start | bytes 2359304 | tf_op jit(solution)/shard_map/ppermute | solution.py:23
  145.6 48.1 %collective-permute-start.11 = (bf16[256,3,128]{2,0,1:T(8,128)(2,1)S(1)}, bf16[256,3,128]{2,0,1:T(8,128)(2,1)S(1)}, u32[]{:S(2)}, u32[]{:S(2)}) collective-permute-start(bf16[256,3,128]{2,0,1:T(8,128)(2,1)S(1)} %get-tuple-element.437), channel_id=1, source_target_pairs={{6,0},{8,2},{10,4},{12,6},{14,8},{16,10},{18,12},{20,14},{22,16},{... | collective-permute-start | bytes 589832 | tf_op jit(solution)/shard_map/ppermute | solution.py:23
  150.6 19.0 %collective-permute-start.9 = (bf16[512,3,128]{2,0,1:T(8,128)(2,1)}, bf16[512,3,128]{2,0,1:T(8,128)(2,1)S(1)}, u32[]{:S(2)}, u32[]{:S(2)}) collective-permute-start(bf16[512,3,128]{2,0,1:T(8,128)(2,1)} %pad_maximum_fusion.4), channel_id=1, source_target_pairs={{2,0},{4,2},{6,4},{8,6},{10,8},{12,10},{14,12},{16,14},{18,16},{20... | collective-permute-start | bytes 1179656 | tf_op jit(solution)/shard_map/ppermute | solution.py:23
  169.6 22.3 %collective-permute-start.10 = (bf16[1024,3,128]{2,0,1:T(8,128)(2,1)}, bf16[1024,3,128]{2,0,1:T(8,128)(2,1)S(1)}, u32[]{:S(2)}, u32[]{:S(2)}) collective-permute-start(bf16[1024,3,128]{2,0,1:T(8,128)(2,1)} %get-tuple-element.435), channel_id=1, source_target_pairs={{4,0},{6,2},{8,4},{10,6},{12,8},{14,10},{16,12},{18,14},{20,16},{2... | collective-permute-start | bytes 2359304 | tf_op jit(solution)/shard_map/ppermute | solution.py:23
  245.4 6.1 copy-start
  317.3 6.0 copy-start
  389.2 6.1 copy-start
  460.9 6.1 copy-start
  509.5 34.0 %collective-permute-start.20 = (bf16[512,3,128]{0,2,1:T(8,128)(2,1)S(1)}, bf16[512,3,128]{0,2,1:T(8,128)(2,1)S(1)}, u32[]{:S(2)}, u32[]{:S(2)}) collective-permute-start(bf16[512,3,128]{0,2,1:T(8,128)(2,1)S(1)} %pad_maximum_fusion.7), channel_id=1, source_target_pairs={{0,2},{2,4},{4,6},{6,8},{8,10},{10,12},{12,14},{14,16},{16,18},{18... | collective-permute-start | bytes 1179656 | tf_op jit(solution)/shard_map/ppermute | solution.py:23
  512.9 46.4 %collective-permute-start.21 = (bf16[512,3,128]{0,2,1:T(8,128)(2,1)}, bf16[512,3,128]{0,2,1:T(8,128)(2,1)}, u32[]{:S(2)}, u32[]{:S(2)}) collective-permute-start(bf16[512,3,128]{0,2,1:T(8,128)(2,1)} %pad_maximum_fusion.8), channel_id=1, source_target_pairs={{2,0},{4,2},{6,4},{8,6},{10,8},{12,10},{14,12},{16,14},{18,16},{20... | collective-permute-start | bytes 1179656 | tf_op jit(solution)/shard_map/ppermute | solution.py:23
  516.8 65.6 %collective-permute-start.19 = (bf16[1024,3,128]{0,2,1:T(8,128)(2,1)}, bf16[1024,3,128]{0,2,1:T(8,128)(2,1)}, u32[]{:S(2)}, u32[]{:S(2)}) collective-permute-start(bf16[1024,3,128]{0,2,1:T(8,128)(2,1)} %get-tuple-element.425), channel_id=1, source_target_pairs={{0,4},{2,6},{4,8},{6,10},{8,12},{10,14},{12,16},{14,18},{16,20},{1... | collective-permute-start | bytes 2359304 | tf_op jit(solution)/shard_map/ppermute | solution.py:23
  521.2 82.0 %collective-permute-start.22 = (bf16[1024,3,128]{0,2,1:T(8,128)(2,1)}, bf16[1024,3,128]{0,2,1:T(8,128)(2,1)}, u32[]{:S(2)}, u32[]{:S(2)}) collective-permute-start(bf16[1024,3,128]{0,2,1:T(8,128)(2,1)} %get-tuple-element.426), channel_id=1, source_target_pairs={{4,0},{6,2},{8,4},{10,6},{12,8},{14,10},{16,12},{18,14},{20,16},{2... | collective-permute-start | bytes 2359304 | tf_op jit(solution)/shard_map/ppermute | solution.py:23
  540.5 21.3 %collective-permute-start.14 = (bf16[512,3,128]{2,0,1:T(8,128)(2,1)}, bf16[512,3,128]{2,0,1:T(8,128)(2,1)}, u32[]{:S(2)}, u32[]{:S(2)}) collective-permute-start(bf16[512,3,128]{2,0,1:T(8,128)(2,1)} %pad_maximum_fusion.5), channel_id=1, source_target_pairs={{0,2},{2,4},{4,6},{6,8},{8,10},{10,12},{12,14},{14,16},{16,18},{18... | collective-permute-start | bytes 1179656 | tf_op jit(solution)/shard_map/ppermute | solution.py:23
  542.7 48.6 %copy-start.3 = (f32[1024,3,128]{2,0,1:T(8,128)S(1)}, f32[1024,3,128]{2,0,1:T(8,128)}, u32[]{:S(2)}) copy-start(f32[1024,3,128]{2,0,1:T(8,128)} %get-tuple-element.370) | copy-start | bytes 4718596
  542.7 48.6 %copy-start.6 = (f32[1024,128]{1,0:T(8,128)S(1)}, f32[1024,128]{1,0:T(8,128)}, u32[]{:S(2)}) copy-start(f32[1024,128]{1,0:T(8,128)} %copy-done.5) | copy-start | bytes 1572868
  542.8 48.6 %copy-start.8 = (f32[1024,128]{1,0:T(8,128)S(1)}, f32[1024,128]{1,0:T(8,128)}, u32[]{:S(2)}) copy-start(f32[1024,128]{1,0:T(8,128)} %get-tuple-element.442) | copy-start | bytes 1572868
  542.8 48.6 %copy-start.15 = (s32[128]{0:T(128)S(1)}, s32[128]{0:T(128)}, u32[]{:S(2)}) copy-start(s32[128]{0:T(128)} %copy-done.14) | copy-start | bytes 1540
  543.6 29.4 %collective-permute-start.15 = (bf16[512,3,128]{2,0,1:T(8,128)(2,1)}, bf16[512,3,128]{2,0,1:T(8,128)(2,1)}, u32[]{:S(2)}, u32[]{:S(2)}) collective-permute-start(bf16[512,3,128]{2,0,1:T(8,128)(2,1)} %pad_maximum_fusion.6), channel_id=1, source_target_pairs={{2,0},{4,2},{6,4},{8,6},{10,8},{12,10},{14,12},{16,14},{18,16},{20... | collective-permute-start | bytes 1179656 | tf_op jit(solution)/shard_map/ppermute | solution.py:23
  552.3 54.2 %all-to-all-start.4 = ((bf16[2,512,384]{2,1,0:T(8,128)(2,1)}), bf16[2,512,384]{2,1,0:T(8,128)(2,1)}, u32[]{:S(2)}, u32[]{:S(2)}) async-start(bf16[2,512,384]{2,1,0:T(8,128)(2,1)} %copy.149), calls=%async_computation.4 | async-start | bytes 1572864 | tf_op jit(solution)/shard_map/all_to_all | solution.py:327
  559.3 60.5 %collective-permute-start.13 = (bf16[1024,3,128]{2,0,1:T(8,128)(2,1)}, bf16[1024,3,128]{2,0,1:T(8,128)(2,1)}, u32[]{:S(2)}, u32[]{:S(2)}) collective-permute-start(bf16[1024,3,128]{2,0,1:T(8,128)(2,1)} %get-tuple-element.433), channel_id=1, source_target_pairs={{0,4},{2,6},{4,8},{6,10},{8,12},{10,14},{12,16},{14,18},{16,20},{1... | collective-permute-start | bytes 2359304 | tf_op jit(solution)/shard_map/ppermute | solution.py:23
  561.9 59.2 %collective-permute-start.16 = (bf16[1024,3,128]{2,0,1:T(8,128)(2,1)}, bf16[1024,3,128]{2,0,1:T(8,128)(2,1)}, u32[]{:S(2)}, u32[]{:S(2)}) collective-permute-start(bf16[1024,3,128]{2,0,1:T(8,128)(2,1)} %get-tuple-element.434), channel_id=1, source_target_pairs={{4,0},{6,2},{8,4},{10,6},{12,8},{14,10},{16,12},{18,14},{20,16},{2... | collective-permute-start | bytes 2359304 | tf_op jit(solution)/shard_map/ppermute | solution.py:23
  573.0 37.9 %collective-permute-start.18 = (bf16[256,3,128]{0,2,1:T(8,128)(2,1)}, bf16[256,3,128]{0,2,1:T(8,128)(2,1)}, u32[]{:S(2)}, u32[]{:S(2)}) collective-permute-start(bf16[256,3,128]{0,2,1:T(8,128)(2,1)} %get-tuple-element.419), channel_id=1, source_target_pairs={{0,6},{2,8},{4,10},{6,12},{8,14},{10,16},{12,18},{14,20},{16,22},{... | collective-permute-start | bytes 589832 | tf_op jit(solution)/shard_map/ppermute | solution.py:23
  582.4 33.7 %collective-permute-start.23 = (bf16[256,3,128]{0,2,1:T(8,128)(2,1)}, bf16[256,3,128]{0,2,1:T(8,128)(2,1)}, u32[]{:S(2)}, u32[]{:S(2)}) collective-permute-start(bf16[256,3,128]{0,2,1:T(8,128)(2,1)} %get-tuple-element.420), channel_id=1, source_target_pairs={{6,0},{8,2},{10,4},{12,6},{14,8},{16,10},{18,12},{20,14},{22,16},{... | collective-permute-start | bytes 589832 | tf_op jit(solution)/shard_map/ppermute | solution.py:23
  593.2 10.1 %copy-start.13 = (bf16[256,3,128]{2,0,1:T(8,128)(2,1)S(1)}, bf16[256,3,128]{2,0,1:T(8,128)(2,1)}, u32[]{:S(2)}) copy-start(bf16[256,3,128]{2,0,1:T(8,128)(2,1)} %get-tuple-element.427) | copy-start | bytes 589828
  598.0 12.8 %copy-start.12 = (bf16[256,3,128]{2,0,1:T(8,128)(2,1)S(1)}, bf16[256,3,128]{2,0,1:T(8,128)(2,1)}, u32[]{:S(2)}) copy-start(bf16[256,3,128]{2,0,1:T(8,128)(2,1)} %get-tuple-element.428) | copy-start | bytes 589828
  603.3 23.4 %collective-permute-start.12 = (bf16[256,3,128]{2,0,1:T(8,128)(2,1)S(1)}, bf16[256,3,128]{2,0,1:T(8,128)(2,1)}, u32[]{:S(2)}, u32[]{:S(2)}) collective-permute-start(bf16[256,3,128]{2,0,1:T(8,128)(2,1)S(1)} %copy-done.13), channel_id=1, source_target_pairs={{0,6},{2,8},{4,10},{6,12},{8,14},{10,16},{12,18},{14,20},{16,22},{... | collective-permute-start | bytes 589832 | tf_op jit(solution)/shard_map/ppermute | solution.py:23
  606.5 15.8 %all-to-all-start.5 = ((bf16[2,512,384]{1,2,0:T(8,128)(2,1)}), bf16[2,512,384]{1,2,0:T(8,128)(2,1)}, u32[]{:S(2)}, u32[]{:S(2)}) async-start(bf16[2,512,384]{1,2,0:T(8,128)(2,1)} %copy.154), calls=%async_computation.5 | async-start | bytes 1572864 | tf_op jit(solution)/shard_map/all_to_all | solution.py:334
  610.9 15.8 %collective-permute-start.17 = (bf16[256,3,128]{2,0,1:T(8,128)(2,1)S(1)}, bf16[256,3,128]{2,0,1:T(8,128)(2,1)}, u32[]{:S(2)}, u32[]{:S(2)}) collective-permute-start(bf16[256,3,128]{2,0,1:T(8,128)(2,1)S(1)} %copy-done.12), channel_id=1, source_target_pairs={{6,0},{8,2},{10,4},{12,6},{14,8},{16,10},{18,12},{20,14},{22,16},{... | collective-permute-start | bytes 589832 | tf_op jit(solution)/shard_map/ppermute | solution.py:23
  622.4 16.5 %all-to-all-start.7 = ((bf16[2,512,384]{2,1,0:T(8,128)(2,1)}), bf16[2,512,384]{2,1,0:T(8,128)(2,1)}, u32[]{:S(2)}, u32[]{:S(2)}) async-start(bf16[2,512,384]{2,1,0:T(8,128)(2,1)} %bitcast.92), calls=%async_computation.7 | async-start | bytes 1572864 | tf_op jit(solution)/shard_map/all_to_all | solution.py:336
  638.9 14.9 %all-to-all-start.6 = ((bf16[2,512,384]{1,2,0:T(8,128)(2,1)}), bf16[2,512,384]{1,2,0:T(8,128)(2,1)S(1)}, u32[]{:S(2)}, u32[]{:S(2)}) async-start(bf16[2,512,384]{1,2,0:T(8,128)(2,1)} %copy.161), calls=%async_computation.6 | async-start | bytes 1572864 | tf_op jit(solution)/shard_map/all_to_all | solution.py:335
  (4 other events, 11.5 us)
where the time goes:
time: 667 us; the launch traced here: 655 us
  local copies, waits for them, and re-layouts  200 us (30%)
  other arithmetic  176 us (26%)
  starting transfers between devices  128 us (19%)
  matrix products  66.6 us (10%)
  waiting for transfers between devices  63.9 us (10%)
  loops' own time  9.58 us (1%)
  blocking collectives  9.09 us (1%)
    dynamic_update_slice x68, other arithmetic, add_near(): lax.dynamic_update_slice_in_dim(band, current + terms[member * TILE_TOK:(...  126 us
    ppermute x24, starting transfers between devices, passed_along(): return lax.ppermute(value, axis, pairs)  95.8 us
    while x104, local copies, waits for them, and re-layouts  67.9 us
    ppermute x24, waiting for transfers between devices, passed_along(): return lax.ppermute(value, axis, pairs)  49.7 us
    unnamed x58, local copies, waits for them, and re-layouts  32.9 us
    dot_general x4, matrix products, query_kernel(): jnp.einsum('hqk,qhd->khd', weights_half, g_tile, preferred_element_type=j...  16.8 us
    dynamic_update_slice x8, local copies, waits for them, and re-layouts, put_tile(): lax.dynamic_update_slice_in_dim(tensor, piece, local_tile * TILE_TOK, axi...  15.3 us
  transfers between devices with their start and end apart: 32, of which 7 were waited for; matrix products, arithmetic and copies ran while one was open for 20% of the time, Pallas kernels for 0%

commit v1 on v0

v1 whole, which is shorter than its diff:
```python
import functools
import math

import jax
import jax.numpy as jnp
from jax import lax
from jax.experimental import pallas as pl
from jax.experimental.pallas import tpu as pltpu
from jax.sharding import PartitionSpec as P

HEAD_DIM = 128
TILE_TOK = 256
GRID_COLS = 8
ROW_TOK = TILE_TOK * GRID_COLS
HALF_TOK = ROW_TOK // 2
BAND_TOK = HALF_TOK + TILE_TOK
THETA = 10000.0
MESH = pl.DeviceIdType.MESH
INV_ROOT = HEAD_DIM ** (-0.5)
VMEM_LIMIT = 56 * 1024 * 1024


def angle_tables(row_ids, col_ids):
    turned = 7 * HEAD_DIM // 16
    unturned = HEAD_DIM - 2 * turned
    slot_ids = lax.iota(jnp.int32, HEAD_DIM)
    offset = slot_ids - unturned
    by_column = offset >= turned
    within = jnp.where(by_column, offset - turned, offset)
    paired = jnp.maximum(within, 0) // 2
    frequency = jnp.exp(paired.astype(jnp.float32) * (-2.0 * math.log(THETA) / turned))
    chosen = jnp.where(by_column[None, :], col_ids[:, None], row_ids[:, None]).astype(jnp.float32)
    angles = chosen * frequency[None, :]
    active = (offset >= 0)[None, :]
    cosine = jnp.where(active, jnp.cos(angles), 1.0)
    parity = jnp.where(within % 2 == 0, -1.0, 1.0)
    signed_sine = jnp.where(active, jnp.sin(angles) * parity[None, :], 0.0)
    return (cosine, signed_sine)


def swapped(x):
    lane = lax.broadcasted_iota(jnp.int32, x.shape, 1)
    after = pltpu.roll(x, HEAD_DIM - 1, 1)
    before = pltpu.roll(x, 1, 1)
    return jnp.where(lane % 2 == 0, after, before)


def pack_kernel(q_ref, k_ref, v_ref, g_ref, cos_ref, sin_ref, packed):
    cosine, sine = cos_ref[...], sin_ref[...]
    for head in range(packed.shape[0]):
        cols = slice(head * HEAD_DIM, (head + 1) * HEAD_DIM)
        for slot, ref in ((0, k_ref), (2, q_ref)):
            x = ref[:, cols].astype(jnp.float32)
            packed[head, slot] = (x * cosine + swapped(x) * sine).astype(jnp.bfloat16)
        packed[head, 1] = v_ref[:, cols]
        packed[head, 3] = g_ref[:, cols]


def unpack_kernel(flag_ref, out_ref, halo_ref, cos_ref, sin_ref, att_ref, dq_ref, dk_ref, dv_ref):
    cosine, sine = cos_ref[...], sin_ref[...]
    heads, _, length, _ = out_ref.shape
    halo_heads, _, piece, _ = halo_ref.shape

    def back(x):
        return (x * cosine + swapped(x * sine)).astype(jnp.bfloat16)

    for head in range(heads):
        cols = slice(head * HEAD_DIM, (head + 1) * HEAD_DIM)
        att_ref[:, cols] = out_ref[head, 2]
        dq_ref[:, cols] = back(out_ref[head, 3].astype(jnp.float32))
        pair = [out_ref[head, i].astype(jnp.float32) for i in range(2)]
        at = head - (heads - halo_heads)
        if at >= 0:
            for i in range(2):
                extra = halo_ref[at, i].astype(jnp.float32)
                first = jnp.where(flag_ref[0] > 0, extra, 0.0)
                last = jnp.where(flag_ref[1] > 0, extra, 0.0)
                if piece == length:
                    pair[i] = pair[i] + first + last
                else:
                    gap = jnp.zeros((length - piece, HEAD_DIM), jnp.float32)
                    pair[i] = (
                        pair[i]
                        + jnp.concatenate([first, gap], axis=0)
                        + jnp.concatenate([gap, last], axis=0)
                    )
        dk_ref[:, cols] = back(pair[0])
        dv_ref[:, cols] = pair[1].astype(jnp.bfloat16)


class Place:
    def __init__(self, head_axis, length):
        self.tile = lax.axis_index("tile")
        self.head = lax.axis_index("head")
        self.heads = head_axis
        self.length = length
        self.piece = min(length, TILE_TOK)
        self.pieces = TILE_TOK // self.piece
        self.plane = self.tile // 4
        self.x = (self.tile // 2) % 2
        self.core = self.tile % 2
        self.pos = self.core * head_axis + self.head
        self.worker = self.x * head_axis + self.head
        self.row = 2 * self.plane + self.core
        self.rows = lax.axis_size("tile") // 2
        self.has_up = self.row > 0
        self.has_down = self.row < self.rows - 1
        self.tile_up = self.tile - 3 + 2 * self.core
        self.tile_down = self.tile + 1 + 2 * self.core

    def worker_at(self, step):
        worker = (self.worker + step) % (2 * self.heads)
        x, head = worker // self.heads, worker % self.heads
        tile = self.plane * 4 + x * 2 + self.x
        here = (tile == self.tile) & (head == self.head)
        return worker, (tile, head), here

    def owner_at(self, step):
        pos = (self.pos + step) % (2 * self.heads)
        core, head = pos // self.heads, pos % self.heads
        tile = self.plane * 4 + self.core * 2 + core
        here = (tile == self.tile) & (head == self.head)
        return pos, core, head, (tile, head), here

    def lends(self, core, head):
        return jnp.where(core == 1, head, self.heads - 1 - head) < self.pieces

    def lent_from(self, core):
        return pl.multiple_of((1 - core) * (self.length - self.piece), self.piece)

    def lent_to(self, core, head):
        low = (head - (self.heads - self.pieces)) * self.piece
        high = HALF_TOK + head * self.piece
        return pl.multiple_of(core * high + (1 - core) * low, self.piece)

    def span(self, start, size=None):
        size = self.length if size is None else size
        return pl.ds(pl.multiple_of(start, self.piece), size)


def move(src, dst, send_sem, recv_sem, device, here):
    remote = pltpu.make_async_remote_copy(
        src_ref=src,
        dst_ref=dst,
        send_sem=send_sem,
        recv_sem=recv_sem,
        device_id=device,
        device_id_type=MESH,
    )

    @pl.when(here)
    def _():
        pltpu.make_async_copy(src, dst, recv_sem).start()

    @pl.when(jnp.logical_not(here))
    def _():
        remote.start()

    return remote


def wait_in(dst, sem):
    pltpu.make_async_copy(dst, dst, sem).wait()


def unless(flag):
    return pl.when(jnp.logical_not(flag))


def greet(place, devices):
    barrier = pltpu.get_barrier_semaphore()

    def tell(device):
        pl.semaphore_signal(barrier, inc=1, device_id=device, device_id_type=MESH)

    for device, here in devices:
        @unless(here)
        def _():
            tell(device)

    @pl.when(place.has_up)
    def _():
        tell((place.tile_up, place.head))

    @pl.when(place.has_down)
    def _():
        tell((place.tile_down, place.head))

    own = (place.x == place.core).astype(jnp.int32)
    ends = place.has_up.astype(jnp.int32) + place.has_down.astype(jnp.int32)
    pl.semaphore_wait(barrier, len(devices) - own + ends)


def gather_kernel(
    head_axis, length, packed, kva, kvb, qga, qgb, send, recv, row_send, row_recv, row_send_b, row_recv_b
):
    place = Place(head_axis, length)
    steps = 2 * head_axis
    greet(place, [place.owner_at(s)[3:5] for s in range(steps)])
    first_b = 2 * head_axis
    sent = []

    def kv_copies(step):
        worker, device, here = place.worker_at(step)
        mine = place.span(place.pos * length)
        head_b = first_b + worker // 2
        side = worker % 2
        copy = move(
            packed.at[worker, pl.ds(0, 2)],
            kva.at[1, :, mine],
            send.at[0, step],
            recv.at[0, place.pos],
            device,
            here,
        )
        sent.append((copy, jnp.logical_not(here)))
        whole = side == place.core
        lent = jnp.logical_not(whole) & place.lends(place.core, place.head)

        @pl.when(whole)
        def _():
            move(
                packed.at[head_b, pl.ds(0, 2)],
                kvb.at[1, :, place.span(place.core * TILE_TOK + place.head * length)],
                send.at[1, step],
                recv.at[1, place.pos],
                device,
                here,
            )

        @pl.when(lent)
        def _():
            move(
                packed.at[head_b, pl.ds(0, 2), pl.ds(place.lent_from(place.core), place.piece)],
                kvb.at[1, :, pl.ds(place.lent_to(place.core, place.head), place.piece)],
                send.at[1, step],
                recv.at[1, place.pos],
                device,
                here,
            )

        return whole, lent

    def qg_copies(step):
        worker, device, here = place.worker_at(step)
        mine = place.span(place.pos * length)
        move(
            packed.at[worker, pl.ds(2, 2)],
            qga.at[:, mine],
            send.at[2, step],
            recv.at[2, place.pos],
            device,
            here,
        )

        @pl.when(worker % 2 == place.core)
        def _():
            move(
                packed.at[first_b + worker // 2, pl.ds(2, 2)],
                qgb.at[:, place.span(place.head * length)],
                send.at[3, step],
                recv.at[3, place.pos],
                device,
                here,
            )

    for step in range(steps):
        kv_copies(step)
    for step in range(steps):
        qg_copies(step)

    side = place.worker % 2

    def pass_on(ref, part, sems_out, sems_in):
        own = ref.at[1] if part is None else ref.at[1, :, part]
        for way, (exists, tile, slot) in enumerate(
            ((place.has_down, place.tile_down, 0), (place.has_up, place.tile_up, 2))
        ):
            there = ref.at[slot] if part is None else ref.at[slot, :, part]
            other = ref.at[2 - slot] if part is None else ref.at[2 - slot, :, part]

            @pl.when(exists)
            def _():
                pltpu.make_async_remote_copy(
                    src_ref=own,
                    dst_ref=there,
                    send_sem=sems_out(way),
                    recv_sem=sems_in(way),
                    device_id=(tile, place.head),
                    device_id_type=MESH,
                ).start()

            @unless(exists)
            def _():
                pltpu.make_async_copy(own, other, sems_in(1 - way)).start()

    for step in range(steps):
        pos, core, head, _, _ = place.owner_at(step)
        part = place.span(pos * length)
        wait_in(kva.at[1, :, part], recv.at[0, pos])
        pass_on(
            kva,
            part,
            lambda way: row_send.at[way, pos],
            lambda way: row_recv.at[way, pos],
        )
    for step in range(steps):
        pos, core, head, _, _ = place.owner_at(step)

        @pl.when(core == side)
        def _():
            wait_in(kvb.at[1, :, place.span(core * TILE_TOK + head * length)], recv.at[1, pos])

        @pl.when((core != side) & place.lends(core, head))
        def _():
            wait_in(kvb.at[1, :, pl.ds(place.lent_to(core, head), place.piece)], recv.at[1, pos])

    pass_on(kvb, None, lambda way: row_send_b.at[way], lambda way: row_recv_b.at[way])

    for step in range(steps):
        pos, core, head, _, _ = place.owner_at(step)
        wait_in(qga.at[:, place.span(pos * length)], recv.at[2, pos])

        @pl.when(core == side)
        def _():
            wait_in(qgb.at[:, place.span(head * length)], recv.at[3, pos])

    for way, slot in enumerate((0, 2)):
        for step in range(steps):
            pos = place.owner_at(step)[0]
            wait_in(kva.at[slot, :, place.span(pos * length)], row_recv.at[way, pos])
        wait_in(kvb.at[slot], row_recv_b.at[way])

        exists = (place.has_down, place.has_up)[way]

        @pl.when(exists)
        def _():
            for step in range(steps):
                pos = place.owner_at(step)[0]
                wait_in(kva.at[1, :, place.span(pos * length)], row_send.at[way, pos])
            wait_in(kvb.at[1], row_send_b.at[way])

    for step in range(steps):
        worker, device, here = place.worker_at(step)
        whole = worker % 2 == place.core
        lent = jnp.logical_not(whole) & place.lends(place.core, place.head)
        head_b = first_b + worker // 2

        @unless(here)
        def _():
            wait_in(packed.at[worker, pl.ds(0, 2)], send.at[0, step])
            wait_in(packed.at[worker, pl.ds(2, 2)], send.at[2, step])

            @pl.when(whole)
            def _():
                wait_in(packed.at[head_b, pl.ds(0, 2)], send.at[1, step])
                wait_in(packed.at[head_b, pl.ds(2, 2)], send.at[3, step])

            @pl.when(lent)
            def _():
                wait_in(
                    packed.at[head_b, pl.ds(0, 2), pl.ds(place.lent_from(place.core), place.piece)],
                    send.at[1, step],
                )


def scatter_kernel(
    head_axis,
    length,
    own_a,
    own_b,
    far_a,
    far_b,
    aqa,
    aqb,
    out,
    halo,
    got_a,
    got_b,
    sum_a,
    sum_b,
    send,
    recv,
    row_send,
    row_recv,
):
    place = Place(head_axis, length)
    steps = 2 * head_axis
    greet(place, [place.worker_at(s)[1:3] for s in range(steps)])
    first_b = 2 * head_axis
    side = place.worker % 2
    head_b = first_b + place.worker // 2

    rows = ((place.has_up, place.tile_up), (place.has_down, place.tile_down))
    for way, (exists, tile) in enumerate(rows):
        for kind, (far, got) in enumerate(((far_a, got_a), (far_b, got_b))):
            @pl.when(exists)
            def _():
                pltpu.make_async_remote_copy(
                    src_ref=far.at[way],
                    dst_ref=got.at[way],
                    send_sem=row_send.at[way, kind],
                    recv_sem=row_recv.at[way, kind],
                    device_id=(tile, place.head),
                    device_id_type=MESH,
                ).start()

            @unless(exists)
            def _():
                pltpu.make_async_copy(
                    far.at[way], got.at[1 - way], row_recv.at[1 - way, kind]
                ).start()

    for step in range(steps):
        pos, core, head, device, here = place.owner_at(step)
        move(
            aqa.at[:, place.span(pos * length)],
            out.at[place.worker, pl.ds(2, 2)],
            send.at[0, step],
            recv.at[0, place.worker],
            device,
            here,
        )

        @pl.when(core == side)
        def _():
            move(
                aqb.at[:, place.span(head * length)],
                out.at[head_b, pl.ds(2, 2)],
                send.at[1, step],
                recv.at[1, place.worker],
                device,
                here,
            )

    for way in range(2):
        for kind, got in enumerate((got_a, got_b)):
            wait_in(got.at[way], row_recv.at[way, kind])

    for own, got, total in ((own_a, got_a, sum_a), (own_b, got_b, sum_b)):
        chunk = TILE_TOK

        def add(i, carry, own=own, got=got, total=total):
            at = pl.ds(pl.multiple_of(i * chunk, chunk), chunk)
            for j in range(2):
                total[j, at] = (
                    own[j, at]
                    + got[0, j, at].astype(jnp.float32)
                    + got[1, j, at].astype(jnp.float32)
                ).astype(jnp.bfloat16)
            return carry

        lax.fori_loop(0, own.shape[1] // chunk, add, 0)

    for step in range(steps):
        pos, core, head, device, here = place.owner_at(step)
        move(
            sum_a.at[:, place.span(pos * length)],
            out.at[place.worker, pl.ds(0, 2)],
            send.at[2, step],
            recv.at[2, place.worker],
            device,
            here,
        )

        @pl.when(core == side)
        def _():
            move(
                sum_b.at[:, place.span(core * TILE_TOK + head * length)],
                out.at[head_b, pl.ds(0, 2)],
                send.at[3, step],
                recv.at[3, place.worker],
                device,
                here,
            )

        @pl.when((core != side) & place.lends(core, head))
        def _():
            move(
                sum_b.at[:, pl.ds(place.lent_to(core, head), place.piece)],
                halo.at[place.worker // 2],
                send.at[3, step],
                recv.at[3, place.worker],
                device,
                here,
            )

    for way, (exists, tile) in enumerate(rows):
        @pl.when(exists)
        def _():
            for kind, far in enumerate((far_a, far_b)):
                wait_in(far.at[way], row_send.at[way, kind])

    for step in range(steps):
        pos, core, head, device, here = place.owner_at(step)
        part = place.span(pos * length)

        @unless(here)
        def _():
            wait_in(aqa.at[:, part], send.at[0, step])
            wait_in(sum_a.at[:, part], send.at[2, step])

            @pl.when(core == side)
            def _():
                wait_in(aqb.at[:, place.span(head * length)], send.at[1, step])
                wait_in(
                    sum_b.at[:, place.span(core * TILE_TOK + head * length)], send.at[3, step]
                )

            @pl.when((core != side) & place.lends(core, head))
            def _():
                wait_in(
                    sum_b.at[:, pl.ds(place.lent_to(core, head), place.piece)], send.at[3, step]
                )

    for step in range(steps):
        worker, _, _ = place.worker_at(step)
        wait_in(out.at[worker, pl.ds(2, 2)], recv.at[0, worker])
        wait_in(out.at[worker, pl.ds(0, 2)], recv.at[2, worker])
        whole = worker % 2 == place.core
        lent = jnp.logical_not(whole) & place.lends(place.core, place.head)

        @pl.when(whole)
        def _():
            wait_in(out.at[first_b + worker // 2, pl.ds(2, 2)], recv.at[1, worker])
            wait_in(out.at[first_b + worker // 2, pl.ds(0, 2)], recv.at[3, worker])

        @pl.when(lent)
        def _():
            wait_in(halo.at[worker // 2], recv.at[3, worker])


BIG = 1e30


def attend_kernel(
    flags, kva, kvb, qga, qgb, aqa, aqb, own_a, own_b, far_a, far_b, trans_a, trans_b, acc_a, acc_b, probs
):
    side = flags[2]
    to_log2 = INV_ROOT / math.log(2.0)
    f32 = jnp.float32
    row_ok = (flags[0] > 0, True, flags[1] > 0)

    for kv, trans, acc in ((kva, trans_a, acc_a), (kvb, trans_b, acc_b)):
        acc[...] = jnp.zeros_like(acc)

        def turn(i, carry, kv=kv, trans=trans):
            at = pl.ds(pl.multiple_of(i * TILE_TOK, TILE_TOK), TILE_TOK)
            for dr in range(3):
                for j in range(2):
                    trans[dr, j, :, at] = kv[dr, j, at].T
            return carry

        lax.fori_loop(0, kv.shape[2] // TILE_TOK, turn, 0)

    def unit(i, col, base, kv, qg, aq, trans, acc):
        band = kv.shape[2] // TILE_TOK
        start = jnp.clip(col - 1 - base, 0, band - 3)
        here = pl.ds(pl.multiple_of(i * TILE_TOK, TILE_TOK), TILE_TOK)
        q, g = qg[0, here], qg[1, here]
        tiles = []
        for dr in range(3):
            for j in range(3):
                at = pl.ds(pl.multiple_of((start + j) * TILE_TOK, TILE_TOK), TILE_TOK)
                away = base + start + j - col
                ok = (away >= -1) & (away <= 1)
                if dr != 1:
                    ok = ok & row_ok[dr]
                tiles.append((dr, at, ok))
        over_lanes = (((1,), (1,)), ((), ()))
        top = jnp.full((1, TILE_TOK), -BIG, f32)
        for n, (dr, at, ok) in enumerate(tiles):
            s = lax.dot_general(kv[dr, 0, at], q, over_lanes, preferred_element_type=f32)
            probs[n] = s
            top = jnp.maximum(top, jnp.where(ok, jnp.max(s, axis=0, keepdims=True), -BIG))
        top = top * to_log2
        total = jnp.zeros((1, TILE_TOK), f32)
        att = jnp.zeros((HEAD_DIM, TILE_TOK), f32)
        for n, (dr, at, ok) in enumerate(tiles):
            p = jnp.exp2(probs[n] * to_log2 - jnp.where(ok, top, BIG))
            probs[n] = p
            total = total + jnp.sum(p, axis=0, keepdims=True)
            att = att + jnp.dot(
                trans[dr, 1, :, at], p.astype(jnp.bfloat16), preferred_element_type=f32
            )
        inverse = 1.0 / total
        att = (att * inverse).astype(jnp.bfloat16)
        aq[0, here] = att.T
        dots = jnp.sum(att.astype(f32) * g.T.astype(f32), axis=0, keepdims=True)
        dq = jnp.zeros((HEAD_DIM, TILE_TOK), f32)
        for n, (dr, at, ok) in enumerate(tiles):
            w = probs[n] * inverse
            dp = lax.dot_general(kv[dr, 1, at], g, over_lanes, preferred_element_type=f32)
            ds = (w * (dp - dots)).astype(jnp.bfloat16)
            acc[dr, 1, at] += jnp.dot(w.astype(jnp.bfloat16), g, preferred_element_type=f32)
            acc[dr, 0, at] += jnp.dot(ds, q, preferred_element_type=f32)
            dq = dq + jnp.dot(trans[dr, 0, :, at], ds, preferred_element_type=f32)
        aq[1, here] = (dq * INV_ROOT).T.astype(jnp.bfloat16)

    def unit_a(i, carry):
        unit(i, i, 0, kva, qga, aqa, trans_a, acc_a)
        return carry

    def unit_b(i, carry):
        unit(i, i + side * (GRID_COLS // 2), side * (GRID_COLS // 2 - 1), kvb, qgb, aqb, trans_b, acc_b)
        return carry

    lax.fori_loop(0, GRID_COLS, unit_a, 0)
    lax.fori_loop(0, GRID_COLS // 2, unit_b, 0)
    for acc, own, far in ((acc_a, own_a, far_a), (acc_b, own_b, far_b)):
        for j, scale in enumerate((INV_ROOT, 1.0)):
            own[j] = acc[1, j] * scale
            far[0, j] = (acc[0, j] * scale).astype(jnp.bfloat16)
            far[1, j] = (acc[2, j] * scale).astype(jnp.bfloat16)


def local(head_axis, queries, keys_in, values_in, grad_out, positions):
    length, width = queries.shape
    heads = width // HEAD_DIM
    bf16, f32 = jnp.bfloat16, jnp.float32
    assert heads == 3 * head_axis and 2 * head_axis * length == ROW_TOK and head_axis % 2 == 0
    place = Place(head_axis, length)
    piece = place.piece
    steps = 2 * head_axis
    cosine, sine = angle_tables(positions[0], positions[1])
    any_space = pl.BlockSpec(memory_space=pl.ANY)
    vmem = pl.BlockSpec(memory_space=pltpu.VMEM)
    smem = pl.BlockSpec(memory_space=pltpu.SMEM)
    shape = jax.ShapeDtypeStruct
    dma = pltpu.SemaphoreType.DMA

    packed = pl.pallas_call(
        pack_kernel,
        out_shape=shape((heads, 4, length, HEAD_DIM), bf16),
        in_specs=[vmem] * 6,
        out_specs=vmem,
        compiler_params=pltpu.CompilerParams(vmem_limit_bytes=VMEM_LIMIT),
    )(queries, keys_in, values_in, grad_out, cosine, sine)

    kva, kvb, qga, qgb = pl.pallas_call(
        functools.partial(gather_kernel, head_axis, length),
        out_shape=(
            shape((3, 2, ROW_TOK, HEAD_DIM), bf16),
            shape((3, 2, BAND_TOK, HEAD_DIM), bf16),
            shape((2, ROW_TOK, HEAD_DIM), bf16),
            shape((2, HALF_TOK, HEAD_DIM), bf16),
        ),
        in_specs=[any_space],
        out_specs=[any_space] * 4,
        scratch_shapes=[
            dma((4, steps)),
            dma((4, steps)),
            dma((2, steps)),
            dma((2, steps)),
            dma((2,)),
            dma((2,)),
        ],
        compiler_params=pltpu.CompilerParams(collective_id=0, has_side_effects=True),
    )(packed)

    flags = jnp.stack(
        [place.has_up.astype(jnp.int32), place.has_down.astype(jnp.int32), place.worker % 2]
    ).astype(jnp.int32)
    aqa, aqb, own_a, own_b, far_a, far_b = pl.pallas_call(
        attend_kernel,
        out_shape=(
            shape((2, ROW_TOK, HEAD_DIM), bf16),
            shape((2, HALF_TOK, HEAD_DIM), bf16),
            shape((2, ROW_TOK, HEAD_DIM), f32),
            shape((2, BAND_TOK, HEAD_DIM), f32),
            shape((2, 2, ROW_TOK, HEAD_DIM), bf16),
            shape((2, 2, BAND_TOK, HEAD_DIM), bf16),
        ),
        in_specs=[smem] + [vmem] * 4,
        out_specs=[vmem] * 6,
        scratch_shapes=[
            pltpu.VMEM((3, 2, HEAD_DIM, ROW_TOK), bf16),
            pltpu.VMEM((3, 2, HEAD_DIM, BAND_TOK), bf16),
            pltpu.VMEM((3, 2, ROW_TOK, HEAD_DIM), f32),
            pltpu.VMEM((3, 2, BAND_TOK, HEAD_DIM), f32),
            pltpu.VMEM((9, TILE_TOK, TILE_TOK), f32),
        ],
        compiler_params=pltpu.CompilerParams(vmem_limit_bytes=VMEM_LIMIT),
    )(flags, kva, kvb, qga, qgb)

    out, halo = pl.pallas_call(
        functools.partial(scatter_kernel, head_axis, length),
        out_shape=(
            shape((heads, 4, length, HEAD_DIM), bf16),
            shape((head_axis, 2, piece, HEAD_DIM), bf16),
        ),
        in_specs=[vmem] * 2 + [any_space] * 4,
        out_specs=[any_space] * 2,
        scratch_shapes=[
            pltpu.VMEM((2, 2, ROW_TOK, HEAD_DIM), bf16),
            pltpu.VMEM((2, 2, BAND_TOK, HEAD_DIM), bf16),
            pltpu.VMEM((2, ROW_TOK, HEAD_DIM), bf16),
            pltpu.VMEM((2, BAND_TOK, HEAD_DIM), bf16),
            dma((4, steps)),
            dma((4, steps)),
            dma((2, 2)),
            dma((2, 2)),
        ],
        compiler_params=pltpu.CompilerParams(
            collective_id=1, has_side_effects=True, vmem_limit_bytes=VMEM_LIMIT
        ),
    )(own_a, own_b, far_a, far_b, aqa, aqb)

    lends = place.lends(place.core, place.head)
    halo_flags = jnp.stack([lends & (place.core == 1), lends & (place.core == 0)]).astype(jnp.int32)
    return pl.pallas_call(
        unpack_kernel,
        out_shape=(shape((length, width), bf16),) * 4,
        in_specs=[smem] + [vmem] * 4,
        out_specs=[vmem] * 4,
        compiler_params=pltpu.CompilerParams(vmem_limit_bytes=VMEM_LIMIT),
    )(halo_flags, out, halo, cosine, sine)


def solution(mesh):
    tokens = P(("tile", "head"), None)
    return jax.shard_map(
        functools.partial(local, mesh.shape["head"]),
        mesh=mesh,
        in_specs=(tokens, tokens, tokens, tokens, P(None, ("tile", "head"))),
        out_specs=(tokens, tokens, tokens, tokens),
        check_vma=False,
    )
```

time: 667 us -> 191 us (0.29)
  the two profiles are of different devices: /device:TPU:16 before, /device:TPU:0 now
where the time goes in v1:
time: 191 us
  Pallas kernels  187 us (98%)
  other arithmetic  3.16 us (2%)
    pallas_call x1, Pallas kernels, local(): pl.pallas_call(functools.partial(gather_kernel, head_axis, length), out_s...  88.9 us
    pallas_call x1, Pallas kernels, local(): pl.pallas_call(attend_kernel, out_shape=(shape((2, ROW_TOK, HEAD_DIM), bf...  45.1 us
    pallas_call x1, Pallas kernels, local(): pl.pallas_call(functools.partial(scatter_kernel, head_axis, length), out_...  42.3 us
    pallas_call x1, Pallas kernels, local(): pl.pallas_call(unpack_kernel, out_shape=(shape((length, width), bf16),) *...  5.3 us
    pallas_call x1, Pallas kernels, local(): pl.pallas_call(pack_kernel, out_shape=shape((heads, 4, length, HEAD_DIM),...  5 us

profile of v1, /device:TPU:0, one launch (start us, length us, event | category | flops | bytes accessed | tf_op | source)
XLA Modules:
  0.0 191.3 jit_solution(15020572108091165092)
XLA Ops:
  0.7 0.7 pad_add_fusion.flags
  1.4 0.6 add_convert_fusion.flag_ref
  2.0 0.8 fusion.3
  2.8 1.9 multiply_select_fusion
  4.6 5.0 %shard_map.84.packed = bf16[6,4,512,128]{3,2,1,0:T(8,128)(2,1)} custom-call(bf16[512,768]{1,0:T(8,128)(2,1)} %q_ref.1, bf16[512,768]{1,0:T(8,128)(2,1)} %k_ref.1, bf16[512,768]{1,0:T(8,128)(2,1)} %v_ref.1, bf16[512,768]{1,0:T(8,128)(2,1)} %g_ref.1, f32[512,128]{1,0:T(8,128)} %get-tuple-element.29.cos_ref, f32[512,128]{1,0:T(8,128)} %get-tuple-element.28.sin_ref), custom_call_target="tpu_custom_call" | custom-call | tf_op jit(solution)/shard_map/pallas_call | solution.py:632
  9.6 88.9 %shard_map.85 = (bf16[3,2,2048,128]{3,2,1,0:T(8,128)(2,1)}, bf16[3,2,1280,128]{3,2,1,0:T(8,128)(2,1)}, bf16[2,2048,128]{2,1,0:T(8,128)(2,1)}, bf16[2,1024,128]{2,1,0:T(8,128)(2,1)}) custom-call(bf16[6,4,512,128]{3,2,1,0:T(8,128)(2,1)} %shard_map.84.packed), custom_call_target="tpu_custom_call" | custom-call | tf_op jit(solution)/shard_map/pallas_call | solution.py:640
  98.6 45.1 %shard_map.86 = (bf16[2,2048,128]{2,1,0:T(8,128)(2,1)}, bf16[2,1024,128]{2,1,0:T(8,128)(2,1)}, f32[2,2048,128]{2,1,0:T(8,128)}, f32[2,1280,128]{2,1,0:T(8,128)},...) custom-call(s32[3]{0:T(128)} %pad_add_fusion.flags, ...), custom_call_target="tpu_custom_call" | custom-call | tf_op jit(solution)/shard_map/pallas_call | solution.py:664
  143.6 42.3 %shard_map.87 = (bf16[6,4,512,128]{3,2,1,0:T(8,128)(2,1)}, bf16[2,2,256,128]{3,2,1,0:T(8,128)(2,1)}) custom-call(f32[2,2048,128]{2,1,0:T(8,128)} %get-tuple-element.20.own_a, f32[2,1280,128]{2,1,0:T(8,128)} %get-tuple-element.21.own_b, bf16[2,2,2048,128]{3,2,1,0:T(8,128)(2,1)} %get-tuple-element.22.far_a, bf16[2,2,1280,128]{3,2,1,0:T(8,128)(2,1)} %get-tuple-element.23.far_b, ...), custom_call_target="tpu_custom_call" | custom-call | tf_op jit(solution)/shard_map/pallas_call | solution.py:686
  186.0 5.3 %shard_map.88 = (bf16[512,768]{1,0:T(8,128)(2,1)}, bf16[512,768]{1,0:T(8,128)(2,1)}, bf16[512,768]{1,0:T(8,128)(2,1)}, bf16[512,768]{1,0:T(8,128)(2,1)}) custom-call(s32[2]{0:T(128)} %add_convert_fusion.flag_ref, bf16[6,4,512,128]{3,2,1,0:T(8,128)(2,1)} %get-tuple-element.26.out_ref, bf16[2,2,256,128]{3,2,1,0:T(8,128)(2,1)} %get-tuple-element.27.halo_ref, ...), custom_call_target="tpu_custom_call" | custom-call | tf_op jit(solution)/shard_map/pallas_call | solution.py:711
  (2 shorter events, 0.0 us)

commit v2 on v1

--- a/solution.py
+++ b/solution.py
@@ -14,6 +14,7 @@
 ROW_TOK = TILE_TOK * GRID_COLS
 HALF_TOK = ROW_TOK // 2
 BAND_TOK = HALF_TOK + TILE_TOK
+WINDOW = 3 * TILE_TOK
 THETA = 10000.0
 MESH = pl.DeviceIdType.MESH
 INV_ROOT = HEAD_DIM ** (-0.5)
@@ -277,7 +278,6 @@
             ((place.has_down, place.tile_down, 0), (place.has_up, place.tile_up, 2))
         ):
             there = ref.at[slot] if part is None else ref.at[slot, :, part]
-            other = ref.at[2 - slot] if part is None else ref.at[2 - slot, :, part]
 
             @pl.when(exists)
             def _():
@@ -290,10 +290,6 @@
                     device_id_type=MESH,
                 ).start()
 
-            @unless(exists)
-            def _():
-                pltpu.make_async_copy(own, other, sems_in(1 - way)).start()
-
     for step in range(steps):
         pos, core, head, _, _ = place.owner_at(step)
         part = place.span(pos * length)
@@ -326,10 +322,12 @@
             wait_in(qgb.at[:, place.span(head * length)], recv.at[3, pos])
 
     for way, slot in enumerate((0, 2)):
-        for step in range(steps):
-            pos = place.owner_at(step)[0]
-            wait_in(kva.at[slot, :, place.span(pos * length)], row_recv.at[way, pos])
-        wait_in(kvb.at[slot], row_recv_b.at[way])
+        @pl.when((place.has_up, place.has_down)[way])
+        def _():
+            for step in range(steps):
+                pos = place.owner_at(step)[0]
+                wait_in(kva.at[slot, :, place.span(pos * length)], row_recv.at[way, pos])
+            wait_in(kvb.at[slot], row_recv_b.at[way])
 
         exists = (place.has_down, place.has_up)[way]
 
@@ -405,12 +403,6 @@
                     device_id_type=MESH,
                 ).start()
 
-            @unless(exists)
-            def _():
-                pltpu.make_async_copy(
-                    far.at[way], got.at[1 - way], row_recv.at[1 - way, kind]
-                ).start()
-
     for step in range(steps):
         pos, core, head, device, here = place.owner_at(step)
         move(
@@ -433,9 +425,15 @@
                 here,
             )
 
-    for way in range(2):
+    for way, exists in enumerate((place.has_down, place.has_up)):
         for kind, got in enumerate((got_a, got_b)):
-            wait_in(got.at[way], row_recv.at[way, kind])
+            @pl.when(exists)
+            def _():
+                wait_in(got.at[way], row_recv.at[way, kind])
+
+            @unless(exists)
+            def _():
+                got[way] = jnp.zeros(got.shape[1:], got.dtype)
 
     for own, got, total in ((own_a, got_a, sum_a), (own_b, got_b, sum_b)):
         chunk = TILE_TOK
@@ -540,6 +538,7 @@
     to_log2 = INV_ROOT / math.log(2.0)
     f32 = jnp.float32
     row_ok = (flags[0] > 0, True, flags[1] > 0)
+    rows = (1 - flags[0], 1, 1 + flags[1])
 
     for kv, trans, acc in ((kva, trans_a, acc_a), (kvb, trans_b, acc_b)):
         acc[...] = jnp.zeros_like(acc)
@@ -548,7 +547,7 @@
             at = pl.ds(pl.multiple_of(i * TILE_TOK, TILE_TOK), TILE_TOK)
             for dr in range(3):
                 for j in range(2):
-                    trans[dr, j, :, at] = kv[dr, j, at].T
+                    trans[dr, j, :, at] = kv[rows[dr], j, at].T
             return carry
 
         lax.fori_loop(0, kv.shape[2] // TILE_TOK, turn, 0)
@@ -557,40 +556,44 @@
         band = kv.shape[2] // TILE_TOK
         start = jnp.clip(col - 1 - base, 0, band - 3)
         here = pl.ds(pl.multiple_of(i * TILE_TOK, TILE_TOK), TILE_TOK)
+        at = pl.ds(pl.multiple_of(start * TILE_TOK, TILE_TOK), WINDOW)
         q, g = qg[0, here], qg[1, here]
-        tiles = []
+        ok = []
         for dr in range(3):
             for j in range(3):
-                at = pl.ds(pl.multiple_of((start + j) * TILE_TOK, TILE_TOK), TILE_TOK)
                 away = base + start + j - col
-                ok = (away >= -1) & (away <= 1)
-                if dr != 1:
-                    ok = ok & row_ok[dr]
-                tiles.append((dr, at, ok))
+                near = (away >= -1) & (away <= 1)
+                ok.append(near if dr == 1 else near & row_ok[dr])
+        parts = [slice(j * TILE_TOK, (j + 1) * TILE_TOK) for j in range(3)]
         over_lanes = (((1,), (1,)), ((), ()))
         top = jnp.full((1, TILE_TOK), -BIG, f32)
-        for n, (dr, at, ok) in enumerate(tiles):
-            s = lax.dot_general(kv[dr, 0, at], q, over_lanes, preferred_element_type=f32)
-            probs[n] = s
-            top = jnp.maximum(top, jnp.where(ok, jnp.max(s, axis=0, keepdims=True), -BIG))
+        for dr in range(3):
+            s = lax.dot_general(kv[rows[dr], 0, at], q, over_lanes, preferred_element_type=f32)
+            probs[dr] = s
+            for j in range(3):
+                best = jnp.max(s[parts[j]], axis=0, keepdims=True)
+                top = jnp.maximum(top, jnp.where(ok[3 * dr + j], best, -BIG))
         top = top * to_log2
         total = jnp.zeros((1, TILE_TOK), f32)
         att = jnp.zeros((HEAD_DIM, TILE_TOK), f32)
-        for n, (dr, at, ok) in enumerate(tiles):
-            p = jnp.exp2(probs[n] * to_log2 - jnp.where(ok, top, BIG))
-            probs[n] = p
-            total = total + jnp.sum(p, axis=0, keepdims=True)
+        for dr in range(3):
+            halves = []
+            for j in range(3):
+                p = jnp.exp2(probs[dr, parts[j]] * to_log2 - jnp.where(ok[3 * dr + j], top, BIG))
+                probs[dr, parts[j]] = p
+                total = total + jnp.sum(p, axis=0, keepdims=True)
+                halves.append(p.astype(jnp.bfloat16))
             att = att + jnp.dot(
-                trans[dr, 1, :, at], p.astype(jnp.bfloat16), preferred_element_type=f32
+                trans[dr, 1, :, at], jnp.concatenate(halves, axis=0), preferred_element_type=f32
             )
         inverse = 1.0 / total
         att = (att * inverse).astype(jnp.bfloat16)
         aq[0, here] = att.T
         dots = jnp.sum(att.astype(f32) * g.T.astype(f32), axis=0, keepdims=True)
         dq = jnp.zeros((HEAD_DIM, TILE_TOK), f32)
-        for n, (dr, at, ok) in enumerate(tiles):
-            w = probs[n] * inverse
-            dp = lax.dot_general(kv[dr, 1, at], g, over_lanes, preferred_element_type=f32)
+        for dr in range(3):
+            w = probs[dr] * inverse
+            dp = lax.dot_general(kv[rows[dr], 1, at], g, over_lanes, preferred_element_type=f32)
             ds = (w * (dp - dots)).astype(jnp.bfloat16)
             acc[dr, 1, at] += jnp.dot(w.astype(jnp.bfloat16), g, preferred_element_type=f32)
             acc[dr, 0, at] += jnp.dot(ds, q, preferred_element_type=f32)
@@ -678,7 +681,7 @@
             pltpu.VMEM((3, 2, HEAD_DIM, BAND_TOK), bf16),
             pltpu.VMEM((3, 2, ROW_TOK, HEAD_DIM), f32),
             pltpu.VMEM((3, 2, BAND_TOK, HEAD_DIM), f32),
-            pltpu.VMEM((9, TILE_TOK, TILE_TOK), f32),
+            pltpu.VMEM((3, WINDOW, TILE_TOK), f32),
         ],
         compiler_params=pltpu.CompilerParams(vmem_limit_bytes=VMEM_LIMIT),
     )(flags, kva, kvb, qga, qgb)

time: 191 us -> 144 us (0.75)
  the two profiles are of different devices: /device:TPU:0 before, /device:TPU:3 now
where the time goes in v2:
time: 144 us; the launch traced here: 143 us
  Pallas kernels  138 us (96%)
  other arithmetic  3.16 us (2%)
    pallas_call x1, Pallas kernels, local(): pl.pallas_call(functools.partial(scatter_kernel, head_axis, length), out_...  48.5 us
    pallas_call x1, Pallas kernels, local(): pl.pallas_call(attend_kernel, out_shape=(shape((2, ROW_TOK, HEAD_DIM), bf...  41.1 us
    pallas_call x1, Pallas kernels, local(): pl.pallas_call(functools.partial(gather_kernel, head_axis, length), out_s...  38.3 us
    pallas_call x1, Pallas kernels, local(): pl.pallas_call(unpack_kernel, out_shape=(shape((length, width), bf16),) *...  5.3 us
    pallas_call x1, Pallas kernels, local(): pl.pallas_call(pack_kernel, out_shape=shape((heads, 4, length, HEAD_DIM),...  5 us

profile of v2, /device:TPU:3, one launch (start us, length us, event | category | flops | bytes accessed | tf_op | source)
XLA Modules:
  0.0 142.9 jit_solution(16725657253581621714)
XLA Ops:
  0.7 0.7 pad_add_fusion.flags
  1.4 0.6 add_convert_fusion.flag_ref
  2.0 0.8 fusion.3
  2.8 1.9 %multiply_select_fusion = (f32[512,128]{1,0:T(8,128)}, f32[512,128]{1,0:T(8,128)}) fusion(f32[128]{0:T(128)S(1)} %get-tuple-element.32, f32[128]{0:T(128)S(1)} %get-tuple-element.33, s32[512]{0:T(512)S(1)} %bitcast.8, s32[512]{0:T(512)S(1)} %bitcast.7, pred[128]{0:T(512)(128)(4,1)S(1)} %get-tuple-element.34, pred[128]{0:T(512)(128)(4,1)S(1)} %get-tuple-element.35), kind=kLoop, calls=%fused_computation | loop fusion | flops 393216 | bytes 529664 | tf_op jit(solution)/shard_map/jit(_where)/select_n | solution.py:38
  4.6 5.0 %shard_map.84.packed = bf16[6,4,512,128]{3,2,1,0:T(8,128)(2,1)} custom-call(bf16[512,768]{1,0:T(8,128)(2,1)} %q_ref.1, bf16[512,768]{1,0:T(8,128)(2,1)} %k_ref.1, bf16[512,768]{1,0:T(8,128)(2,1)} %v_ref.1, bf16[512,768]{1,0:T(8,128)(2,1)} %g_ref.1, f32[512,128]{1,0:T(8,128)} %get-tuple-element.29.cos_ref, f32[512,128]{1,0:T(8,128)} %get-tuple-element.28.sin_ref), custom_call_target="tpu_custom_call" | custom-call | tf_op jit(solution)/shard_map/pallas_call | solution.py:635
  9.6 38.3 %shard_map.85 = (bf16[3,2,2048,128]{3,2,1,0:T(8,128)(2,1)}, bf16[3,2,1280,128]{3,2,1,0:T(8,128)(2,1)}, bf16[2,2048,128]{2,1,0:T(8,128)(2,1)}, bf16[2,1024,128]{2,1,0:T(8,128)(2,1)}) custom-call(bf16[6,4,512,128]{3,2,1,0:T(8,128)(2,1)} %shard_map.84.packed), custom_call_target="tpu_custom_call" | custom-call | tf_op jit(solution)/shard_map/pallas_call | solution.py:643
  47.9 41.1 %shard_map.86 = (bf16[2,2048,128]{2,1,0:T(8,128)(2,1)}, bf16[2,1024,128]{2,1,0:T(8,128)(2,1)}, f32[2,2048,128]{2,1,0:T(8,128)}, f32[2,1280,128]{2,1,0:T(8,128)},...) custom-call(s32[3]{0:T(128)} %pad_add_fusion.flags, ...), custom_call_target="tpu_custom_call" | custom-call | tf_op jit(solution)/shard_map/pallas_call | solution.py:667
  89.0 48.5 %shard_map.87 = (bf16[6,4,512,128]{3,2,1,0:T(8,128)(2,1)}, bf16[2,2,256,128]{3,2,1,0:T(8,128)(2,1)}) custom-call(f32[2,2048,128]{2,1,0:T(8,128)} %get-tuple-element.20.own_a, f32[2,1280,128]{2,1,0:T(8,128)} %get-tuple-element.21.own_b, bf16[2,2,2048,128]{3,2,1,0:T(8,128)(2,1)} %get-tuple-element.22.far_a, bf16[2,2,1280,128]{3,2,1,0:T(8,128)(2,1)} %get-tuple-element.23.far_b, ...), custom_call_target="tpu_custom_call" | custom-call | tf_op jit(solution)/shard_map/pallas_call | solution.py:689
  137.6 5.3 %shard_map.88 = (bf16[512,768]{1,0:T(8,128)(2,1)}, bf16[512,768]{1,0:T(8,128)(2,1)}, bf16[512,768]{1,0:T(8,128)(2,1)}, bf16[512,768]{1,0:T(8,128)(2,1)}) custom-call(s32[2]{0:T(128)} %add_convert_fusion.flag_ref, bf16[6,4,512,128]{3,2,1,0:T(8,128)(2,1)} %get-tuple-element.26.out_ref, bf16[2,2,256,128]{3,2,1,0:T(8,128)(2,1)} %get-tuple-element.27.halo_ref, ...), custom_call_target="tpu_custom_call" | custom-call | tf_op jit(solution)/shard_map/pallas_call | solution.py:714
  (2 shorter events, 0.0 us)

commit v3 on v1

v3 whole, which is shorter than its diff:
```python
import functools
import math

import jax
import jax.numpy as jnp
from jax import lax
from jax.experimental import pallas as pl
from jax.experimental.pallas import tpu as pltpu
from jax.sharding import PartitionSpec as P

HEAD_DIM = 128
TILE_TOK = 256
GRID_COLS = 8
ROW_TOK = TILE_TOK * GRID_COLS
HALF_TOK = ROW_TOK // 2
BAND_TOK = HALF_TOK + TILE_TOK
WINDOW = 3 * TILE_TOK
THETA = 10000.0
MESH = pl.DeviceIdType.MESH
INV_ROOT = HEAD_DIM ** (-0.5)
VMEM_LIMIT = 56 * 1024 * 1024


def angle_tables(row_ids, col_ids):
    turned = 7 * HEAD_DIM // 16
    unturned = HEAD_DIM - 2 * turned
    slot_ids = lax.iota(jnp.int32, HEAD_DIM)
    offset = slot_ids - unturned
    by_column = offset >= turned
    within = jnp.where(by_column, offset - turned, offset)
    paired = jnp.maximum(within, 0) // 2
    frequency = jnp.exp(paired.astype(jnp.float32) * (-2.0 * math.log(THETA) / turned))
    chosen = jnp.where(by_column[None, :], col_ids[:, None], row_ids[:, None]).astype(jnp.float32)
    angles = chosen * frequency[None, :]
    active = (offset >= 0)[None, :]
    cosine = jnp.where(active, jnp.cos(angles), 1.0)
    parity = jnp.where(within % 2 == 0, -1.0, 1.0)
    signed_sine = jnp.where(active, jnp.sin(angles) * parity[None, :], 0.0)
    return (cosine, signed_sine)


def swapped(x):
    lane = lax.broadcasted_iota(jnp.int32, x.shape, 1)
    after = pltpu.roll(x, HEAD_DIM - 1, 1)
    before = pltpu.roll(x, 1, 1)
    return jnp.where(lane % 2 == 0, after, before)


def pack_kernel(q_ref, k_ref, v_ref, g_ref, cos_ref, sin_ref, packed):
    cosine, sine = cos_ref[...], sin_ref[...]
    for head in range(packed.shape[0]):
        cols = slice(head * HEAD_DIM, (head + 1) * HEAD_DIM)
        for slot, ref in ((0, k_ref), (2, q_ref)):
            x = ref[:, cols].astype(jnp.float32)
            packed[head, slot] = (x * cosine + swapped(x) * sine).astype(jnp.bfloat16)
        packed[head, 1] = v_ref[:, cols]
        packed[head, 3] = g_ref[:, cols]


def unpack_kernel(flag_ref, out_ref, halo_ref, cos_ref, sin_ref, att_ref, dq_ref, dk_ref, dv_ref):
    cosine, sine = cos_ref[...], sin_ref[...]
    heads, _, length, _ = out_ref.shape
    halo_heads, _, piece, _ = halo_ref.shape

    def back(x):
        return (x * cosine + swapped(x * sine)).astype(jnp.bfloat16)

    for head in range(heads):
        cols = slice(head * HEAD_DIM, (head + 1) * HEAD_DIM)
        att_ref[:, cols] = out_ref[head, 2]
        dq_ref[:, cols] = back(out_ref[head, 3].astype(jnp.float32))
        pair = [out_ref[head, i].astype(jnp.float32) for i in range(2)]
        at = head - (heads - halo_heads)
        if at >= 0:
            for i in range(2):
                extra = halo_ref[at, i].astype(jnp.float32)
                first = jnp.where(flag_ref[0] > 0, extra, 0.0)
                last = jnp.where(flag_ref[1] > 0, extra, 0.0)
                if piece == length:
                    pair[i] = pair[i] + first + last
                else:
                    gap = jnp.zeros((length - piece, HEAD_DIM), jnp.float32)
                    pair[i] = (
                        pair[i]
                        + jnp.concatenate([first, gap], axis=0)
                        + jnp.concatenate([gap, last], axis=0)
                    )
        dk_ref[:, cols] = back(pair[0])
        dv_ref[:, cols] = pair[1].astype(jnp.bfloat16)


class Place:
    def __init__(self, head_axis, length):
        self.tile = lax.axis_index("tile")
        self.head = lax.axis_index("head")
        self.heads = head_axis
        self.length = length
        self.piece = min(length, TILE_TOK)
        self.pieces = TILE_TOK // self.piece
        self.plane = self.tile // 4
        self.x = (self.tile // 2) % 2
        self.core = self.tile % 2
        self.pos = self.core * head_axis + self.head
        self.worker = self.x * head_axis + self.head
        self.row = 2 * self.plane + self.core
        self.rows = lax.axis_size("tile") // 2
        self.has_up = self.row > 0
        self.has_down = self.row < self.rows - 1
        self.tile_up = self.tile - 3 + 2 * self.core
        self.tile_down = self.tile + 1 + 2 * self.core

    def worker_at(self, step):
        worker = (self.worker + step) % (2 * self.heads)
        x, head = worker // self.heads, worker % self.heads
        tile = self.plane * 4 + x * 2 + self.x
        here = (tile == self.tile) & (head == self.head)
        return worker, (tile, head), here

    def owner_at(self, step):
        pos = (self.pos + step) % (2 * self.heads)
        core, head = pos // self.heads, pos % self.heads
        tile = self.plane * 4 + self.core * 2 + core
        here = (tile == self.tile) & (head == self.head)
        return pos, core, head, (tile, head), here

    def lends(self, core, head):
        return jnp.where(core == 1, head, self.heads - 1 - head) < self.pieces

    def lent_from(self, core):
        return pl.multiple_of((1 - core) * (self.length - self.piece), self.piece)

    def lent_to(self, core, head):
        low = (head - (self.heads - self.pieces)) * self.piece
        high = HALF_TOK + head * self.piece
        return pl.multiple_of(core * high + (1 - core) * low, self.piece)

    def span(self, start, size=None):
        size = self.length if size is None else size
        return pl.ds(pl.multiple_of(start, self.piece), size)


def move(src, dst, send_sem, recv_sem, device, here):
    remote = pltpu.make_async_remote_copy(
        src_ref=src,
        dst_ref=dst,
        send_sem=send_sem,
        recv_sem=recv_sem,
        device_id=device,
        device_id_type=MESH,
    )

    @pl.when(here)
    def _():
        pltpu.make_async_copy(src, dst, recv_sem).start()

    @pl.when(jnp.logical_not(here))
    def _():
        remote.start()

    return remote


def wait_in(dst, sem):
    pltpu.make_async_copy(dst, dst, sem).wait()


def unless(flag):
    return pl.when(jnp.logical_not(flag))


def greet(place, devices):
    barrier = pltpu.get_barrier_semaphore()

    def tell(device):
        pl.semaphore_signal(barrier, inc=1, device_id=device, device_id_type=MESH)

    for device, here in devices:
        @unless(here)
        def _():
            tell(device)

    @pl.when(place.has_up)
    def _():
        tell((place.tile_up, place.head))

    @pl.when(place.has_down)
    def _():
        tell((place.tile_down, place.head))

    own = (place.x == place.core).astype(jnp.int32)
    ends = place.has_up.astype(jnp.int32) + place.has_down.astype(jnp.int32)
    pl.semaphore_wait(barrier, len(devices) - 2 * own + ends)


BIG = 1e30


def attend_kernel(
    head_axis,
    length,
    packed,
    out,
    halo,
    kva,
    kvb,
    qga,
    qgb,
    aqa,
    aqb,
    far_a,
    far_b,
    got_a,
    got_b,
    sum_a,
    sum_b,
    trans_a,
    trans_b,
    acc_a,
    acc_b,
    probs,
    send,
    recv,
    row_send,
    row_recv,
    row_send_b,
    row_recv_b,
    back_send,
    back_recv,
    ret_send,
    ret_recv,
):
    place = Place(head_axis, length)
    steps = 2 * head_axis
    first_b = 2 * head_axis
    greet(
        place,
        [place.owner_at(s)[3:5] for s in range(steps)]
        + [place.worker_at(s)[1:3] for s in range(steps)],
    )
    side = place.worker % 2
    head_b = first_b + place.worker // 2
    to_log2 = INV_ROOT / math.log(2.0)
    f32 = jnp.float32
    row_ok = (place.has_up, True, place.has_down)
    up = (place.row + place.rows - 1) // place.rows
    down = 1 - place.row // (place.rows - 1)
    rows = (1 - up, 1, 1 + down)

    def kv_a_copies(step):
        worker, device, here = place.worker_at(step)
        mine = place.span(place.pos * length)
        move(
            packed.at[worker, pl.ds(0, 2)],
            kva.at[1, :, mine],
            send.at[0, step],
            recv.at[0, place.pos],
            device,
            here,
        )
    def kv_b_copies(step):
        worker, device, here = place.worker_at(step)
        head_b = first_b + worker // 2
        whole = worker % 2 == place.core
        lent = jnp.logical_not(whole) & place.lends(place.core, place.head)

        @pl.when(whole)
        def _():
            move(
                packed.at[head_b, pl.ds(0, 2)],
                kvb.at[1, :, place.span(place.core * TILE_TOK + place.head * length)],
                send.at[1, step],
                recv.at[1, place.pos],
                device,
                here,
            )

        @pl.when(lent)
        def _():
            move(
                packed.at[head_b, pl.ds(0, 2), pl.ds(place.lent_from(place.core), place.piece)],
                kvb.at[1, :, pl.ds(place.lent_to(place.core, place.head), place.piece)],
                send.at[1, step],
                recv.at[1, place.pos],
                device,
                here,
            )

    def qg_a_copies(step):
        worker, device, here = place.worker_at(step)
        mine = place.span(place.pos * length)
        move(
            packed.at[worker, pl.ds(2, 2)],
            qga.at[:, mine],
            send.at[2, step],
            recv.at[2, place.pos],
            device,
            here,
        )

    def qg_b_copies(step):
        worker, device, here = place.worker_at(step)

        @pl.when(worker % 2 == place.core)
        def _():
            move(
                packed.at[first_b + worker // 2, pl.ds(2, 2)],
                qgb.at[:, place.span(place.head * length)],
                send.at[3, step],
                recv.at[3, place.pos],
                device,
                here,
            )

    for copies in (kv_a_copies, qg_a_copies, kv_b_copies, qg_b_copies):
        for step in range(steps):
            copies(step)

    for acc in (acc_a, acc_b):
        acc[...] = jnp.zeros_like(acc)

    def pass_on(ref, part, sems_out, sems_in):
        own = ref.at[1] if part is None else ref.at[1, :, part]
        for way, (exists, tile, slot) in enumerate(
            ((place.has_down, place.tile_down, 0), (place.has_up, place.tile_up, 2))
        ):
            there = ref.at[slot] if part is None else ref.at[slot, :, part]

            @pl.when(exists)
            def _():
                pltpu.make_async_remote_copy(
                    src_ref=own,
                    dst_ref=there,
                    send_sem=sems_out(way),
                    recv_sem=sems_in(way),
                    device_id=(tile, place.head),
                    device_id_type=MESH,
                ).start()

    for step in range(steps):
        pos, core, head, _, _ = place.owner_at(step)
        part = place.span(pos * length)
        wait_in(kva.at[1, :, part], recv.at[0, pos])
        pass_on(
            kva,
            part,
            lambda way: row_send.at[way, pos],
            lambda way: row_recv.at[way, pos],
        )

    def turn(kv, trans, dr):
        def step_of(i, carry):
            at = pl.ds(pl.multiple_of(i * TILE_TOK, TILE_TOK), TILE_TOK)
            for j in range(2):
                trans[dr, j, :, at] = kv[rows[dr], j, at].T
            return carry

        lax.fori_loop(0, kv.shape[2] // TILE_TOK, step_of, 0)

    turn(kva, trans_a, 1)
    for step in range(steps):
        pos = place.owner_at(step)[0]
        wait_in(qga.at[:, place.span(pos * length)], recv.at[2, pos])
    for way, slot in enumerate((0, 2)):
        @pl.when((place.has_up, place.has_down)[way])
        def _():
            for step in range(steps):
                pos = place.owner_at(step)[0]
                wait_in(kva.at[slot, :, place.span(pos * length)], row_recv.at[way, pos])

    turn(kva, trans_a, 0)
    turn(kva, trans_a, 2)

    def unit(i, start, col, base, kv, qg, aq, trans, acc):
        here = pl.ds(pl.multiple_of(i * TILE_TOK, TILE_TOK), TILE_TOK)
        at = pl.ds(pl.multiple_of(start * TILE_TOK, TILE_TOK), WINDOW)
        q, g = qg[0, here], qg[1, here]
        ok = []
        for dr in range(3):
            for j in range(3):
                away = base + start + j - col
                near = (away >= -1) & (away <= 1)
                ok.append(near if dr == 1 else near & row_ok[dr])
        parts = [slice(j * TILE_TOK, (j + 1) * TILE_TOK) for j in range(3)]
        over_lanes = (((1,), (1,)), ((), ()))
        top = jnp.full((1, TILE_TOK), -BIG, f32)
        for dr in range(3):
            s = lax.dot_general(kv[rows[dr], 0, at], q, over_lanes, preferred_element_type=f32)
            probs[dr] = s
            for j in range(3):
                best = jnp.max(s[parts[j]], axis=0, keepdims=True)
                top = jnp.maximum(top, jnp.where(ok[3 * dr + j], best, -BIG))
        top = top * to_log2
        total = jnp.zeros((1, TILE_TOK), f32)
        att = jnp.zeros((HEAD_DIM, TILE_TOK), f32)
        for dr in range(3):
            halves = []
            for j in range(3):
                p = jnp.exp2(probs[dr, parts[j]] * to_log2 - jnp.where(ok[3 * dr + j], top, BIG))
                probs[dr, parts[j]] = p
                total = total + jnp.sum(p, axis=0, keepdims=True)
                halves.append(p.astype(jnp.bfloat16))
            att = att + jnp.dot(
                trans[dr, 1, :, at], jnp.concatenate(halves, axis=0), preferred_element_type=f32
            )
        inverse = 1.0 / total
        att = (att * inverse).astype(jnp.bfloat16)
        aq[0, here] = att.T
        dots = jnp.sum(att.astype(f32) * g.T.astype(f32), axis=0, keepdims=True)
        dq = jnp.zeros((HEAD_DIM, TILE_TOK), f32)
        for dr in range(3):
            w = probs[dr] * inverse
            dp = lax.dot_general(kv[rows[dr], 1, at], g, over_lanes, preferred_element_type=f32)
            ds = (w * (dp - dots)).astype(jnp.bfloat16)
            acc[dr, 1, at] += jnp.dot(w.astype(jnp.bfloat16), g, preferred_element_type=f32)
            acc[dr, 0, at] += jnp.dot(ds, q, preferred_element_type=f32)
            dq = dq + jnp.dot(trans[dr, 0, :, at], ds, preferred_element_type=f32)
        aq[1, here] = (dq * INV_ROOT).T.astype(jnp.bfloat16)

    def unit_a(i, carry):
        last = GRID_COLS - 1
        start = i - 1 + (last - i) // last - i // last
        unit(i, start, i, 0, kva, qga, aqa, trans_a, acc_a)
        return carry

    def unit_b(i, carry):
        last = GRID_COLS // 2 - 1
        start = i - 1 + side + (1 - side) * ((last - i) // last) - side * (i // last)
        col = i + side * (GRID_COLS // 2)
        unit(i, start, col, side * last, kvb, qgb, aqb, trans_b, acc_b)
        return carry

    ways = ((place.has_up, place.tile_up), (place.has_down, place.tile_down))

    def return_rows(kind, acc, far, got):
        for way in range(2):
            for j, scale in enumerate((INV_ROOT, 1.0)):
                far[way, j] = (acc[2 * way, j] * scale).astype(jnp.bfloat16)
        for way, (exists, tile) in enumerate(ways):
            @pl.when(exists)
            def _():
                pltpu.make_async_remote_copy(
                    src_ref=far.at[way],
                    dst_ref=got.at[way],
                    send_sem=ret_send.at[way, kind],
                    recv_sem=ret_recv.at[way, kind],
                    device_id=(tile, place.head),
                    device_id_type=MESH,
                ).start()

    def add_rows(kind, acc, got, total):
        for way, exists in enumerate((place.has_down, place.has_up)):
            @pl.when(exists)
            def _():
                wait_in(got.at[way], ret_recv.at[way, kind])

            @unless(exists)
            def _():
                got[way] = jnp.zeros(got.shape[1:], got.dtype)

        def add(i, carry):
            at = pl.ds(pl.multiple_of(i * TILE_TOK, TILE_TOK), TILE_TOK)
            for j, scale in enumerate((INV_ROOT, 1.0)):
                total[j, at] = (
                    acc[1, j, at] * scale
                    + got[0, j, at].astype(f32)
                    + got[1, j, at].astype(f32)
                ).astype(jnp.bfloat16)
            return carry

        lax.fori_loop(0, total.shape[1] // TILE_TOK, add, 0)

    def send_back_a(source, at, kind):
        for step in range(steps):
            pos, core, head, device, here = place.owner_at(step)
            move(
                source.at[:, place.span(pos * length)],
                out.at[place.worker, pl.ds(at, 2)],
                back_send.at[kind, step],
                back_recv.at[kind, place.worker],
                device,
                here,
            )

    lax.fori_loop(0, GRID_COLS // 2, unit_a, 0)
    for step in range(steps):
        pos, core, head, _, _ = place.owner_at(step)

        @pl.when(core == side)
        def _():
            wait_in(kvb.at[1, :, place.span(core * TILE_TOK + head * length)], recv.at[1, pos])

        @pl.when((core != side) & place.lends(core, head))
        def _():
            wait_in(kvb.at[1, :, pl.ds(place.lent_to(core, head), place.piece)], recv.at[1, pos])

    pass_on(kvb, None, lambda way: row_send_b.at[way], lambda way: row_recv_b.at[way])

    lax.fori_loop(GRID_COLS // 2, GRID_COLS, unit_a, 0)
    return_rows(0, acc_a, far_a, got_a)
    send_back_a(aqa, 2, 0)

    for step in range(steps):
        pos, core, head, _, _ = place.owner_at(step)

        @pl.when(core == side)
        def _():
            wait_in(qgb.at[:, place.span(head * length)], recv.at[3, pos])

    for way, slot in enumerate((0, 2)):
        @pl.when((place.has_up, place.has_down)[way])
        def _():
            wait_in(kvb.at[slot], row_recv_b.at[way])

    for dr in range(3):
        turn(kvb, trans_b, dr)
    lax.fori_loop(0, GRID_COLS // 2 - 1, unit_b, 0)
    add_rows(0, acc_a, got_a, sum_a)
    send_back_a(sum_a, 0, 2)
    lax.fori_loop(GRID_COLS // 2 - 1, GRID_COLS // 2, unit_b, 0)
    return_rows(1, acc_b, far_b, got_b)

    for step in range(steps):
        pos, core, head, device, here = place.owner_at(step)

        @pl.when(core == side)
        def _():
            move(
                aqb.at[:, place.span(head * length)],
                out.at[head_b, pl.ds(2, 2)],
                back_send.at[1, step],
                back_recv.at[1, place.worker],
                device,
                here,
            )

    add_rows(1, acc_b, got_b, sum_b)
    for step in range(steps):
        pos, core, head, device, here = place.owner_at(step)

        @pl.when(core == side)
        def _():
            move(
                sum_b.at[:, place.span(core * TILE_TOK + head * length)],
                out.at[head_b, pl.ds(0, 2)],
                back_send.at[3, step],
                back_recv.at[3, place.worker],
                device,
                here,
            )

        @pl.when((core != side) & place.lends(core, head))
        def _():
            move(
                sum_b.at[:, pl.ds(place.lent_to(core, head), place.piece)],
                halo.at[place.worker // 2],
                back_send.at[3, step],
                back_recv.at[3, place.worker],
                device,
                here,
            )

    for way, exists in enumerate((place.has_down, place.has_up)):
        @pl.when(exists)
        def _():
            for step in range(steps):
                pos = place.owner_at(step)[0]
                wait_in(kva.at[1, :, place.span(pos * length)], row_send.at[way, pos])
            wait_in(kvb.at[1], row_send_b.at[way])

    for step in range(steps):
        worker, device, here = place.worker_at(step)
        whole = worker % 2 == place.core
        lent = jnp.logical_not(whole) & place.lends(place.core, place.head)
        head_w = first_b + worker // 2

        @unless(here)
        def _():
            wait_in(packed.at[worker, pl.ds(0, 2)], send.at[0, step])
            wait_in(packed.at[worker, pl.ds(2, 2)], send.at[2, step])

            @pl.when(whole)
            def _():
                wait_in(packed.at[head_w, pl.ds(0, 2)], send.at[1, step])
                wait_in(packed.at[head_w, pl.ds(2, 2)], send.at[3, step])

            @pl.when(lent)
            def _():
                wait_in(
                    packed.at[head_w, pl.ds(0, 2), pl.ds(place.lent_from(place.core), place.piece)],
                    send.at[1, step],
                )

    for way, (exists, tile) in enumerate(ways):
        @pl.when(exists)
        def _():
            for kind, far in enumerate((far_a, far_b)):
                wait_in(far.at[way], ret_send.at[way, kind])

    for step in range(steps):
        pos, core, head, device, here = place.owner_at(step)
        part = place.span(pos * length)

        @unless(here)
        def _():
            wait_in(aqa.at[:, part], back_send.at[0, step])
            wait_in(sum_a.at[:, part], back_send.at[2, step])

            @pl.when(core == side)
            def _():
                wait_in(aqb.at[:, place.span(head * length)], back_send.at[1, step])
                wait_in(
                    sum_b.at[:, place.span(core * TILE_TOK + head * length)], back_send.at[3, step]
                )

            @pl.when((core != side) & place.lends(core, head))
            def _():
                wait_in(
                    sum_b.at[:, pl.ds(place.lent_to(core, head), place.piece)], back_send.at[3, step]
                )

    for step in range(steps):
        worker, _, _ = place.worker_at(step)
        wait_in(out.at[worker, pl.ds(2, 2)], back_recv.at[0, worker])
        wait_in(out.at[worker, pl.ds(0, 2)], back_recv.at[2, worker])
        whole = worker % 2 == place.core
        lent = jnp.logical_not(whole) & place.lends(place.core, place.head)

        @pl.when(whole)
        def _():
            wait_in(out.at[first_b + worker // 2, pl.ds(2, 2)], back_recv.at[1, worker])
            wait_in(out.at[first_b + worker // 2, pl.ds(0, 2)], back_recv.at[3, worker])

        @pl.when(lent)
        def _():
            wait_in(halo.at[worker // 2], back_recv.at[3, worker])


def local(head_axis, queries, keys_in, values_in, grad_out, positions):
    length, width = queries.shape
    heads = width // HEAD_DIM
    bf16, f32 = jnp.bfloat16, jnp.float32
    assert heads == 3 * head_axis and 2 * head_axis * length == ROW_TOK and head_axis % 2 == 0
    place = Place(head_axis, length)
    piece = place.piece
    steps = 2 * head_axis
    cosine, sine = angle_tables(positions[0], positions[1])
    any_space = pl.BlockSpec(memory_space=pl.ANY)
    vmem = pl.BlockSpec(memory_space=pltpu.VMEM)
    smem = pl.BlockSpec(memory_space=pltpu.SMEM)
    shape = jax.ShapeDtypeStruct
    dma = pltpu.SemaphoreType.DMA

    packed = pl.pallas_call(
        pack_kernel,
        out_shape=shape((heads, 4, length, HEAD_DIM), bf16),
        in_specs=[vmem] * 6,
        out_specs=vmem,
        compiler_params=pltpu.CompilerParams(vmem_limit_bytes=VMEM_LIMIT),
    )(queries, keys_in, values_in, grad_out, cosine, sine)

    out, halo = pl.pallas_call(
        functools.partial(attend_kernel, head_axis, length),
        out_shape=(
            shape((heads, 4, length, HEAD_DIM), bf16),
            shape((head_axis, 2, piece, HEAD_DIM), bf16),
        ),
        in_specs=[any_space],
        out_specs=[any_space] * 2,
        scratch_shapes=[
            pltpu.VMEM((3, 2, ROW_TOK, HEAD_DIM), bf16),
            pltpu.VMEM((3, 2, BAND_TOK, HEAD_DIM), bf16),
            pltpu.VMEM((2, ROW_TOK, HEAD_DIM), bf16),
            pltpu.VMEM((2, HALF_TOK, HEAD_DIM), bf16),
            pltpu.VMEM((2, ROW_TOK, HEAD_DIM), bf16),
            pltpu.VMEM((2, HALF_TOK, HEAD_DIM), bf16),
            pltpu.VMEM((2, 2, ROW_TOK, HEAD_DIM), bf16),
            pltpu.VMEM((2, 2, BAND_TOK, HEAD_DIM), bf16),
            pltpu.VMEM((2, 2, ROW_TOK, HEAD_DIM), bf16),
            pltpu.VMEM((2, 2, BAND_TOK, HEAD_DIM), bf16),
            pltpu.VMEM((2, ROW_TOK, HEAD_DIM), bf16),
            pltpu.VMEM((2, BAND_TOK, HEAD_DIM), bf16),
            pltpu.VMEM((3, 2, HEAD_DIM, ROW_TOK), bf16),
            pltpu.VMEM((3, 2, HEAD_DIM, BAND_TOK), bf16),
            pltpu.VMEM((3, 2, ROW_TOK, HEAD_DIM), f32),
            pltpu.VMEM((3, 2, BAND_TOK, HEAD_DIM), f32),
            pltpu.VMEM((3, WINDOW, TILE_TOK), f32),
            dma((4, steps)),
            dma((4, steps)),
            dma((2, steps)),
            dma((2, steps)),
            dma((2,)),
            dma((2,)),
            dma((4, steps)),
            dma((4, steps)),
            dma((2, 2)),
            dma((2, 2)),
        ],
        compiler_params=pltpu.CompilerParams(
            collective_id=0, has_side_effects=True, vmem_limit_bytes=VMEM_LIMIT
        ),
    )(packed)

    lends = place.lends(place.core, place.head)
    halo_flags = jnp.stack([lends & (place.core == 1), lends & (place.core == 0)]).astype(jnp.int32)
    return pl.pallas_call(
        unpack_kernel,
        out_shape=(shape((length, width), bf16),) * 4,
        in_specs=[smem] + [vmem] * 4,
        out_specs=[vmem] * 4,
        compiler_params=pltpu.CompilerParams(vmem_limit_bytes=VMEM_LIMIT),
    )(halo_flags, out, halo, cosine, sine)


def solution(mesh):
    tokens = P(("tile", "head"), None)
    return jax.shard_map(
        functools.partial(local, mesh.shape["head"]),
        mesh=mesh,
        in_specs=(tokens, tokens, tokens, tokens, P(None, ("tile", "head"))),
        out_specs=(tokens, tokens, tokens, tokens),
        check_vma=False,
    )
```

time: 191 us -> 108 us (0.57)
  the two profiles are of different devices: /device:TPU:0 before, /device:TPU:3 now
where the time goes in v3:
time: 108 us
  Pallas kernels  104 us (96%)
  other arithmetic  2.55 us (2%)
    pallas_call x1, Pallas kernels, local(): pl.pallas_call(functools.partial(attend_kernel, head_axis, length), out_s...  93.2 us
    pallas_call x1, Pallas kernels, local(): pl.pallas_call(unpack_kernel, out_shape=(shape((length, width), bf16),) *...  5.3 us
    pallas_call x1, Pallas kernels, local(): pl.pallas_call(pack_kernel, out_shape=shape((heads, 4, length, HEAD_DIM),...  4.99 us

profile of v3, /device:TPU:3, one launch (start us, length us, event | category | flops | bytes accessed | tf_op | source)
XLA Modules:
  0.0 107.5 jit_solution(6175404273658667305)
XLA Ops:
  0.7 0.7 add_convert_fusion.flag_ref
  1.3 0.8 fusion.3
  2.1 1.9 %multiply_select_fusion = (f32[512,128]{1,0:T(8,128)}, f32[512,128]{1,0:T(8,128)}) fusion(f32[128]{0:T(128)S(1)} %get-tuple-element.12, f32[128]{0:T(128)S(1)} %get-tuple-element.13, s32[512]{0:T(512)S(1)} %bitcast.5, s32[512]{0:T(512)S(1)} %bitcast.4, pred[128]{0:T(512)(128)(4,1)S(1)} %get-tuple-element.14, pred[128]{0:T(512)(128)(4,1)S(1)} %get-tuple-element.15), kind=kLoop, calls=%fused_computation | loop fusion | flops 393216 | bytes 529664 | tf_op jit(solution)/shard_map/jit(_where)/select_n | solution.py:38
  4.0 5.0 %shard_map.84.packed = bf16[6,4,512,128]{3,2,1,0:T(8,128)(2,1)} custom-call(bf16[512,768]{1,0:T(8,128)(2,1)} %q_ref.1, bf16[512,768]{1,0:T(8,128)(2,1)} %k_ref.1, bf16[512,768]{1,0:T(8,128)(2,1)} %v_ref.1, bf16[512,768]{1,0:T(8,128)(2,1)} %g_ref.1, f32[512,128]{1,0:T(8,128)} %get-tuple-element.9.cos_ref, f32[512,128]{1,0:T(8,128)} %get-tuple-element.8.sin_ref), custom_call_target="tpu_custom_call" | custom-call | tf_op jit(solution)/shard_map/pallas_call | solution.py:653
  9.0 93.2 %shard_map.85 = (bf16[6,4,512,128]{3,2,1,0:T(8,128)(2,1)}, bf16[2,2,256,128]{3,2,1,0:T(8,128)(2,1)}) custom-call(bf16[6,4,512,128]{3,2,1,0:T(8,128)(2,1)} %shard_map.84.packed), custom_call_target="tpu_custom_call" | custom-call | tf_op jit(solution)/shard_map/pallas_call | solution.py:661
  102.2 5.3 %shard_map.86 = (bf16[512,768]{1,0:T(8,128)(2,1)}, bf16[512,768]{1,0:T(8,128)(2,1)}, bf16[512,768]{1,0:T(8,128)(2,1)}, bf16[512,768]{1,0:T(8,128)(2,1)}) custom-call(s32[2]{0:T(128)} %add_convert_fusion.flag_ref, bf16[6,4,512,128]{3,2,1,0:T(8,128)(2,1)} %get-tuple-element.6.out_ref, bf16[2,2,256,128]{3,2,1,0:T(8,128)(2,1)} %get-tuple-element.7.halo_ref, ...), custom_call_target="tpu_custom_call" | custom-call | tf_op jit(solution)/shard_map/pallas_call | solution.py:705
  (2 shorter events, 0.0 us)

commit v4 on v3

--- a/solution.py
+++ b/solution.py
@@ -48,45 +48,39 @@
 
 def pack_kernel(q_ref, k_ref, v_ref, g_ref, cos_ref, sin_ref, packed):
     cosine, sine = cos_ref[...], sin_ref[...]
-    for head in range(packed.shape[0]):
-        cols = slice(head * HEAD_DIM, (head + 1) * HEAD_DIM)
-        for slot, ref in ((0, k_ref), (2, q_ref)):
-            x = ref[:, cols].astype(jnp.float32)
-            packed[head, slot] = (x * cosine + swapped(x) * sine).astype(jnp.bfloat16)
-        packed[head, 1] = v_ref[:, cols]
-        packed[head, 3] = g_ref[:, cols]
+    for slot, ref in ((0, k_ref), (2, q_ref)):
+        x = ref[...].astype(jnp.float32)
+        packed[0, slot] = (x * cosine + swapped(x) * sine).astype(jnp.bfloat16)
+    packed[0, 1] = v_ref[...]
+    packed[0, 3] = g_ref[...]
 
 
 def unpack_kernel(flag_ref, out_ref, halo_ref, cos_ref, sin_ref, att_ref, dq_ref, dk_ref, dv_ref):
     cosine, sine = cos_ref[...], sin_ref[...]
-    heads, _, length, _ = out_ref.shape
-    halo_heads, _, piece, _ = halo_ref.shape
+    length, piece = out_ref.shape[2], halo_ref.shape[2]
 
     def back(x):
         return (x * cosine + swapped(x * sine)).astype(jnp.bfloat16)
 
-    for head in range(heads):
-        cols = slice(head * HEAD_DIM, (head + 1) * HEAD_DIM)
-        att_ref[:, cols] = out_ref[head, 2]
-        dq_ref[:, cols] = back(out_ref[head, 3].astype(jnp.float32))
-        pair = [out_ref[head, i].astype(jnp.float32) for i in range(2)]
-        at = head - (heads - halo_heads)
-        if at >= 0:
-            for i in range(2):
-                extra = halo_ref[at, i].astype(jnp.float32)
-                first = jnp.where(flag_ref[0] > 0, extra, 0.0)
-                last = jnp.where(flag_ref[1] > 0, extra, 0.0)
-                if piece == length:
-                    pair[i] = pair[i] + first + last
-                else:
-                    gap = jnp.zeros((length - piece, HEAD_DIM), jnp.float32)
-                    pair[i] = (
-                        pair[i]
-                        + jnp.concatenate([first, gap], axis=0)
-                        + jnp.concatenate([gap, last], axis=0)
-                    )
-        dk_ref[:, cols] = back(pair[0])
-        dv_ref[:, cols] = pair[1].astype(jnp.bfloat16)
+    shared = pl.program_id(0) >= flag_ref[2]
+    att_ref[...] = out_ref[0, 2]
+    dq_ref[...] = back(out_ref[0, 3].astype(jnp.float32))
+    pair = [out_ref[0, i].astype(jnp.float32) for i in range(2)]
+    for i in range(2):
+        extra = halo_ref[0, i].astype(jnp.float32)
+        first = jnp.where(shared & (flag_ref[0] > 0), extra, 0.0)
+        last = jnp.where(shared & (flag_ref[1] > 0), extra, 0.0)
+        if piece == length:
+            pair[i] = pair[i] + first + last
+        else:
+            gap = jnp.zeros((length - piece, HEAD_DIM), jnp.float32)
+            pair[i] = (
+                pair[i]
+                + jnp.concatenate([first, gap], axis=0)
+                + jnp.concatenate([gap, last], axis=0)
+            )
+    dk_ref[...] = back(pair[0])
+    dv_ref[...] = pair[1].astype(jnp.bfloat16)
 
 
 class Place:
@@ -645,7 +639,8 @@
     steps = 2 * head_axis
     cosine, sine = angle_tables(positions[0], positions[1])
     any_space = pl.BlockSpec(memory_space=pl.ANY)
-    vmem = pl.BlockSpec(memory_space=pltpu.VMEM)
+    by_head = pl.BlockSpec((length, HEAD_DIM), lambda h: (0, h))
+    table = pl.BlockSpec((length, HEAD_DIM), lambda h: (0, 0))
     smem = pl.BlockSpec(memory_space=pltpu.SMEM)
     shape = jax.ShapeDtypeStruct
     dma = pltpu.SemaphoreType.DMA
@@ -653,8 +648,9 @@
     packed = pl.pallas_call(
         pack_kernel,
         out_shape=shape((heads, 4, length, HEAD_DIM), bf16),
-        in_specs=[vmem] * 6,
-        out_specs=vmem,
+        grid=(heads,),
+        in_specs=[by_head] * 4 + [table] * 2,
+        out_specs=pl.BlockSpec((1, 4, length, HEAD_DIM), lambda h: (h, 0, 0, 0)),
         compiler_params=pltpu.CompilerParams(vmem_limit_bytes=VMEM_LIMIT),
     )(queries, keys_in, values_in, grad_out, cosine, sine)
 
@@ -701,12 +697,22 @@
     )(packed)
 
     lends = place.lends(place.core, place.head)
-    halo_flags = jnp.stack([lends & (place.core == 1), lends & (place.core == 0)]).astype(jnp.int32)
+    first_b = heads - head_axis
+    halo_flags = jnp.stack(
+        [lends & (place.core == 1), lends & (place.core == 0), jnp.int32(first_b)]
+    ).astype(jnp.int32)
     return pl.pallas_call(
         unpack_kernel,
         out_shape=(shape((length, width), bf16),) * 4,
-        in_specs=[smem] + [vmem] * 4,
-        out_specs=[vmem] * 4,
+        grid=(heads,),
+        in_specs=[
+            smem,
+            pl.BlockSpec((1, 4, length, HEAD_DIM), lambda h: (h, 0, 0, 0)),
+            pl.BlockSpec((1, 2, piece, HEAD_DIM), lambda h: (jnp.maximum(h - first_b, 0), 0, 0, 0)),
+            table,
+            table,
+        ],
+        out_specs=[by_head] * 4,
         compiler_params=pltpu.CompilerParams(vmem_limit_bytes=VMEM_LIMIT),
     )(halo_flags, out, halo, cosine, sine)
 

time: 108 us -> 110 us (1.019)
  Pallas kernels: 104 us -> 106 us
    pallas_call x1, Pallas kernels: 4.99 us -> 6.3 us  [local(): pl.pallas_call(pack_kernel, out_shape=shape((heads, 4, length, HEAD_DIM),...]
where the time goes in v4:
time: 110 us
  Pallas kernels  106 us (96%)
  other arithmetic  2.55 us (2%)
    pallas_call x1, Pallas kernels, local(): pl.pallas_call(functools.partial(attend_kernel, head_axis, length), out_s...  93.3 us
    pallas_call x1, Pallas kernels, local(): pl.pallas_call(pack_kernel, out_shape=shape((heads, 4, length, HEAD_DIM),...  6.3 us
    pallas_call x1, Pallas kernels, local(): pl.pallas_call(unpack_kernel, out_shape=(shape((length, width), bf16),) *...  6.06 us

profile of v4, /device:TPU:3, one launch (start us, length us, event | category | flops | bytes accessed | tf_op | source)
XLA Modules:
  0.0 109.7 jit_solution(9234490875385459284)
XLA Ops:
  0.7 0.7 pad_add_fusion.flag_ref
  1.3 0.8 fusion.3
  2.1 1.9 %multiply_select_fusion = (f32[512,128]{1,0:T(8,128)}, f32[512,128]{1,0:T(8,128)}) fusion(f32[128]{0:T(128)S(1)} %get-tuple-element.12, f32[128]{0:T(128)S(1)} %get-tuple-element.13, s32[512]{0:T(512)S(1)} %bitcast.5, s32[512]{0:T(512)S(1)} %bitcast.4, pred[128]{0:T(512)(128)(4,1)S(1)} %get-tuple-element.14, pred[128]{0:T(512)(128)(4,1)S(1)} %get-tuple-element.15), kind=kLoop, calls=%fused_computation | loop fusion | flops 393216 | bytes 529664 | tf_op jit(solution)/shard_map/jit(_where)/select_n | solution.py:38
  4.0 6.3 %shard_map.84.packed = bf16[6,4,512,128]{3,2,1,0:T(8,128)(2,1)} custom-call(bf16[512,768]{1,0:T(8,128)(2,1)} %q_ref.1, bf16[512,768]{1,0:T(8,128)(2,1)} %k_ref.1, bf16[512,768]{1,0:T(8,128)(2,1)} %v_ref.1, bf16[512,768]{1,0:T(8,128)(2,1)} %g_ref.1, f32[512,128]{1,0:T(8,128)} %get-tuple-element.9.cos_ref, f32[512,128]{1,0:T(8,128)} %get-tuple-element.8.sin_ref), custom_call_target="tpu_custom_call" | custom-call | tf_op jit(solution)/shard_map/pallas_call | solution.py:648
  10.3 93.3 %shard_map.85 = (bf16[6,4,512,128]{3,2,1,0:T(8,128)(2,1)}, bf16[2,2,256,128]{3,2,1,0:T(8,128)(2,1)}) custom-call(bf16[6,4,512,128]{3,2,1,0:T(8,128)(2,1)} %shard_map.84.packed), custom_call_target="tpu_custom_call" | custom-call | tf_op jit(solution)/shard_map/pallas_call | solution.py:657
  103.6 6.1 %shard_map.86 = (bf16[512,768]{1,0:T(8,128)(2,1)}, bf16[512,768]{1,0:T(8,128)(2,1)}, bf16[512,768]{1,0:T(8,128)(2,1)}, bf16[512,768]{1,0:T(8,128)(2,1)}) custom-call(s32[3]{0:T(128)} %pad_add_fusion.flag_ref, bf16[6,4,512,128]{3,2,1,0:T(8,128)(2,1)} %get-tuple-element.6.out_ref, bf16[2,2,256,128]{3,2,1,0:T(8,128)(2,1)} %get-tuple-element.7.halo_ref, ...), custom_call_target="tpu_custom_call" | custom-call | tf_op jit(solution)/shard_map/pallas_call | solution.py:704
  (2 shorter events, 0.0 us)
